TPU v7x, 256 devices: a whole 4x4x8 slice. The times are simulated.
256 devices in a mesh: sec: 4 (over x), en: 64 (over y, z, core).
Axes of the slice: x: 4, y: 4, z: 8, core: 2. Of those that a mesh axis runs over, the one named last changes fastest.
Arguments:
- inverse_blocks: float32 [4, 256, 2, 256, 256], P('sec', 'en')
- coupling: float32 [4, 256, 256], P('sec'), may hold values from -0.375 to 0.375
- boundary: float32 [256, 2, 256, 256], P('en')
- band_offsets: int32 [6], replicated, may hold values from -2 to 2, as said below
- band_weights: float32 [4, 6], P('sec'), may hold values from 0.1 to 1
Outputs:
- green_blocks: float32 [4, 256, 2, 256, 256], P('sec', 'en')
- self_energy: float32 [4, 256, 2, 256, 256], P('sec', 'en')
Inputs may be any that keep to these rules, and one draw needn't show every extreme that they name: `band_offsets`: every offset lies within -2 to 2, and both ends occur in every draw.
All inputs are finite; a program needn't handle non-finite values.
Results may differ from a plain program's by a relative error of at most 0.00011.
Values sent between devices are 32-bit elements; how exact they have to be, the bound alone decides.
No kernel may reach another device: no remote copies, remote signals or barrier semaphores. Data moves between devices by JAX's collectives and lax.ppermute only.
A program may use at most 128 MiB of HBM per device.

v0:
```python
import jax
import jax.numpy as jnp
from jax import lax
from jax.experimental import pallas as pl
from jax.experimental.pallas import tpu as pltpu
from jax.sharding import PartitionSpec as P

F32 = jnp.float32
BF16 = jnp.bfloat16
NN = (((1,), (0,)), ((), ()))
NT = (((1,), (1,)), ((), ()))
VMEM = pl.BlockSpec(memory_space=pltpu.VMEM)
SMEM = pl.BlockSpec(memory_space=pltpu.SMEM)
HBM = pl.BlockSpec(memory_space=pltpu.HBM)
PARAMS = pltpu.CompilerParams(vmem_limit_bytes=36 * 1024 * 1024)
SMALL = pltpu.CompilerParams(vmem_limit_bytes=8 * 1024 * 1024)
def split(value):
    high = value.astype(BF16)
    return high, (value - high.astype(F32)).astype(BF16)


def dot3(left, right, dims):
    def one(a, b):
        return lax.dot_general(a, b, dims, preferred_element_type=F32)

    return one(left[0], right[0]) + (one(left[0], right[1]) + one(left[1], right[0]))


def triple(real, imag):
    return split(real), split(imag), split(real + imag)


def gauss(left, right, dims):
    first, second, third = (dot3(a, b, dims) for a, b in zip(left, right))
    return first - second, third - first - second


def store_transfer(inverse, coupling, high, low, stage):
    orb = coupling.shape[-1]
    both = dot3(split(inverse.reshape(2 * orb, orb)), split(coupling), NN)
    for number, (upper, lower) in enumerate(triple(both[:orb], both[orb:])):
        high[stage, number] = upper
        low[stage, number] = lower


def pick_kernel(me, inverse_all, boundary_all, kept, start, sems):
    copies = [
        pltpu.make_async_copy(inverse_all.at[me[0]], kept, sems.at[0]),
        pltpu.make_async_copy(boundary_all.at[me[0]], start, sems.at[1]),
    ]
    for copy in copies:
        copy.start()
    for copy in copies:
        copy.wait()


def run_pick(me, inverse_blocks, boundary):
    block = jax.ShapeDtypeStruct(inverse_blocks.shape[1:], F32)
    return pl.pallas_call(
        pick_kernel,
        out_shape=[block] * 2,
        in_specs=[SMEM] + [HBM] * 2,
        out_specs=[VMEM] * 2,
        scratch_shapes=[pltpu.SemaphoreType.DMA((2,))],
        compiler_params=SMALL,
        name="pick",
    )(me, inverse_blocks, boundary)


def chain_kernel(batch, parts, me_ref, core_ref, quarter_ref, kept, start, own_coupling, *refs):
    arrived = refs[: parts - 1]
    quarters = refs[parts - 1 : 2 * parts - 1]
    outs = refs[2 * parts - 1 : 3 * parts - 1]
    high, low, inverse, previous, coupling = refs[3 * parts - 1 :]
    me = me_ref[0]
    orb = coupling.shape[-1]
    rows = orb // len(quarters)

    @pl.when(lax.rem(me // 2 + core_ref[0], 2) == batch)
    def _():
        coupling[0] = own_coupling[0]
        for number, source in enumerate(quarters):
            quarter = lax.bitwise_xor(quarter_ref[0], number)
            place = pl.ds(pl.multiple_of(quarter * rows, rows), rows)
            for shift in range(1, parts):
                coupling[shift, place, :] = source[shift - 1]
        for shift in range(parts):
            stage = lax.rem(me - shift + parts, parts)
            inverse[stage] = kept[...] if shift == 0 else arrived[shift - 1][0]
            store_transfer(inverse[stage], coupling[shift], high, low, stage)
        previous[...] = start[...]
        for stage in range(parts):
            transfer = [(high[stage, number], low[stage, number]) for number in range(3)]
            half = gauss(transfer, triple(previous[0], previous[1]), NN)
            real, imag = gauss(triple(*half), transfer, NT)
            real = real + inverse[stage, 0]
            imag = imag + inverse[stage, 1]
            if stage < parts - 1:
                previous[0] = real
                previous[1] = imag
            target = lax.rem(stage - me + parts, parts)
            for number in range(parts):

                @pl.when(target == number)
                def _():
                    outs[number][0, 0] = real
                    outs[number][0, 1] = imag


def run_chain(batch, me, core, quarter, kept, start, coupling, arrived, quarters):
    parts = len(arrived) + 1
    orb = start.shape[-1]
    return pl.pallas_call(
        lambda *refs: chain_kernel(batch, parts, *refs),
        out_shape=[jax.ShapeDtypeStruct((1, 2, orb, orb), F32)] * parts,
        in_specs=[SMEM] * 3 + [VMEM] * (3 + len(arrived) + len(quarters)),
        out_specs=[VMEM] * parts,
        scratch_shapes=[
            pltpu.VMEM((parts, 3, orb, orb), BF16),
            pltpu.VMEM((parts, 3, orb, orb), BF16),
            pltpu.VMEM((parts, 2, orb, orb), F32),
            pltpu.VMEM((2, orb, orb), F32),
            pltpu.VMEM((parts, orb, orb), F32),
        ],
        compiler_params=PARAMS,
        cost_estimate=pl.CostEstimate(
            flops=parts * 48 * orb**3,
            bytes_accessed=parts * 20 * orb * orb,
            transcendentals=0,
        ),
        name="chain",
    )(me, core, quarter, kept, start, coupling, *arrived, *quarters)


def pack_kernel(batch, parts, me_ref, core_ref, *refs):
    sources, packed = refs[:parts], refs[parts]
    side = lax.bitwise_xor(core_ref[0], batch)
    for number in range(parts // 2):
        energy = side * (parts // 2) + number
        shift = lax.rem(me_ref[0] - energy + parts, parts)
        for which in range(parts):

            @pl.when(shift == which)
            def _():
                packed[number] = sources[which][0]


def run_pack(batch, me, core, sources):
    parts = len(sources)
    return pl.pallas_call(
        lambda *refs: pack_kernel(batch, parts, *refs),
        out_shape=jax.ShapeDtypeStruct((parts // 2,) + sources[0].shape[1:], F32),
        in_specs=[SMEM] * 2 + [VMEM] * parts,
        out_specs=VMEM,
        compiler_params=SMALL,
        name="pack",
    )(me, core, *sources)


def mix(weights, row, columns, values):
    total = weights[row, columns[0]] * values[0]
    for column, value in zip(columns[1:], values[1:]):
        total = total + weights[row, column] * value
    return total


ROWS = 32


def own_kernel(count, core_ref, weights, far, near, green, partial, sems):
    pair = count // 2
    orb = partial.shape[-1]
    core = core_ref[0]
    copies = []
    for number, (packed, base) in enumerate(((far, core * pair), (near, (1 - core) * pair))):
        copies.append(pltpu.make_async_copy(packed, green.at[pl.ds(base, pair)], sems.at[number]))
        copies[-1].start()
    for half in range(2):

        @pl.loop(0, orb // ROWS)
        def _(step):
            place = pl.ds(pl.multiple_of(step * ROWS, ROWS), ROWS)
            values = [ref[other, half, place, :] for ref in (far, near) for other in range(pair)]
            for row in range(count):
                partial[row, half, place, :] = mix(weights, row, (0, 1, 4, 5), values)

    for copy in copies:
        copy.wait()


def run_own(core, weights, far, near):
    count = weights.shape[0]
    whole = jax.ShapeDtypeStruct((count,) + far.shape[1:], F32)
    return pl.pallas_call(
        lambda *refs: own_kernel(count, *refs),
        out_shape=[whole] * 2,
        in_specs=[SMEM, SMEM, VMEM, VMEM],
        out_specs=[HBM, VMEM],
        scratch_shapes=[pltpu.SemaphoreType.DMA((2,))],
        compiler_params=SMALL,
        name="band_own",
    )(core, weights, far, near)


def admit_kernel(value, kept):
    pass


def run_admit(value):
    return pl.pallas_call(
        admit_kernel,
        out_shape=jax.ShapeDtypeStruct(value.shape, F32),
        in_specs=[VMEM],
        out_specs=VMEM,
        input_output_aliases={0: 0},
        compiler_params=SMALL,
        cost_estimate=pl.CostEstimate(flops=3_000_000_000, bytes_accessed=0, transcendentals=0),
        name="admit",
    )(value)


def halo_kernel(count, core_ref, weights, partial, near, far, energy, done, sems):
    pair = count // 2
    orb = partial.shape[-1]
    copies = []
    for halo, side, columns in ((near, 1 - core_ref[0], (6, 7)), (far, core_ref[0], (2, 3))):
        for number in range(pair):
            row = side * pair + number
            for half in range(2):

                @pl.loop(0, orb // ROWS)
                def _(step):
                    place = pl.ds(pl.multiple_of(step * ROWS, ROWS), ROWS)
                    values = [halo[other, half, place, :] for other in range(pair)]
                    done[row, half, place, :] = partial[row, half, place, :] + mix(
                        weights, row, columns, values
                    )

            copy = pltpu.make_async_copy(done.at[row], energy.at[row], sems.at[len(copies)])
            copy.start()
            copies.append(copy)
    for copy in copies:
        copy.wait()


def run_halo(core, weights, partial, near, far):
    count = weights.shape[0]
    return pl.pallas_call(
        lambda *refs: halo_kernel(count, *refs),
        out_shape=jax.ShapeDtypeStruct(partial.shape, F32),
        in_specs=[SMEM, SMEM, VMEM, VMEM, VMEM],
        out_specs=HBM,
        scratch_shapes=[pltpu.VMEM(partial.shape, F32), pltpu.SemaphoreType.DMA((count,))],
        compiler_params=SMALL,
        name="band_halo",
    )(core, weights, partial, near, far)


def on_device(inverse_blocks, coupling, boundary, band_offsets, band_weights):
    parts, devices = lax.axis_size("sec"), lax.axis_size("en")
    own_inverse = inverse_blocks[0]
    count = own_inverse.shape[0]
    pair = count // 2
    me, lane = lax.axis_index("sec"), lax.axis_index("en")
    orb = coupling.shape[-1]
    rows = orb // 4
    core = lax.rem(lane, 2)
    quarter = core + 2 * lax.rem(lane // 2 + lane // 16, 2)
    both = ("sec", "en")

    def ring(value, shift):
        pairs = [(source, (source + shift) % parts) for source in range(parts)]
        return lax.ppermute(value, "sec", pairs)

    def batch_pairs(batch, shift, to_runner):
        pairs = []
        for runner in range(parts):
            other = (runner - shift) % parts if to_runner else (runner + shift) % parts
            for en in range(devices):
                if (runner // 2 + en) % 2 == batch:
                    near, far = runner * devices + en, other * devices + en
                    pairs.append((far, near) if to_runner else (near, far))
        return pairs

    piece = lax.dynamic_slice(coupling, (0, quarter * rows, 0), (1, rows, orb))
    gathered = [ring(piece, shift) for shift in range(1, parts)]
    sent = [
        lax.dynamic_slice_in_dim(own_inverse, lax.rem(me + shift, parts), 1, axis=0)
        for shift in range(1, parts)
    ]
    def after(values, *waits):
        return list(lax.optimization_barrier((tuple(values), waits))[0])

    first = jnp.concatenate(gathered, axis=0)
    arrived = [
        [
            lax.ppermute(value, both, batch_pairs(batch, shift, True))
            for shift, value in enumerate(values, 1)
        ]
        for batch, values in enumerate((sent, sent))
    ]
    partners = (0, 1, 2, 17)
    quarters = [first] + [
        lax.ppermute(first, "en", [(source, source ^ partner) for source in range(devices)])
        for partner in partners[1:]
    ]
    kept, start = run_pick(me[None], own_inverse, boundary)

    packed = []
    for batch in range(2):
        produced = run_chain(
            batch, me[None], core[None], quarter[None], kept, start, coupling, arrived[batch], quarters
        )
        returned = [produced[0]] + [
            lax.ppermute(produced[shift], both, batch_pairs(batch, shift, False))
            for shift in range(1, parts)
        ]
        returned = after(returned, *packed)
        packed.append(run_pack(batch, me[None], core[None], returned))
    across = []
    for source in range(devices):
        target = source + 1 if source % 2 else source - 1
        if 0 <= target < devices:
            across.append((source, target))
    far_halo = lax.ppermute(packed[0], "en", across)
    near_halo = lax.ppermute(packed[1], "en", [(source, source ^ 1) for source in range(devices)])

    lower = jnp.arange(pair, dtype=jnp.int32)
    a_place, b_place = core * pair + lower, (1 - core) * pair + lower
    a_halo = jnp.where(core == 0, lower - pair, lower + count)
    b_halo = jnp.where(core == 0, lower + count, lower - pair)
    place = jnp.concatenate([a_place, a_halo, b_place, b_halo])
    away = place[None, :] - jnp.arange(count, dtype=jnp.int32)[:, None]
    hits = (band_offsets[:, None, None] == away[None]).astype(F32)
    weights = jnp.sum(band_weights[0][:, None, None] * hits, axis=0)
    core = core[None]
    green, partial = run_own(core, weights, *packed)
    energy = run_halo(core, weights, partial, near_halo, run_admit(far_halo))
    return green[None], energy[None]


def solution(mesh):
    return jax.shard_map(
        on_device,
        mesh=mesh,
        in_specs=(
            P("sec", "en", None, None, None),
            P("sec", None, None),
            P("en", None, None, None),
            P(),
            P("sec", None),
        ),
        out_specs=(P("sec", "en", None, None, None), P("sec", "en", None, None, None)),
        check_vma=False,
    )
```

profile of v0, /device:TPU:14, one launch (start us, length us, event | category | flops | bytes accessed | tf_op | source)
XLA Modules:
  0.0 84.1 jit_solution(8336606965050700849)
XLA Ops:
  2.1 2.4 %collective-permute-start.4 = (f32[1,64,256]{2,1,0:T(8,128)S(1)}, f32[1,64,256]{2,1,0:T(8,128)S(1)}, u32[]{:S(2)}, u32[]{:S(2)}) collective-permute-start(f32[1,64,256]{2,1,0:T(8,128)S(1)} %constant_dynamic-slice_fusion), channel_id=1, source_target_pairs={{0,128},{64,192},{128,0},{192,64},{1,129},{65,193},{129,1},{193,65... | collective-permute-start | bytes 196616 | tf_op jit(solution)/shard_map/ppermute | solution.py:273
  4.6 1.5 %dynamic-slice_bitcast_fusion = (f32[1,2,256,256]{3,2,1,0:T(8,128)S(1)}, f32[1,2,256,256]{3,2,1,0:T(8,128)S(1)}, f32[1,2,256,256]{3,2,1,0:T(8,128)S(1)}) fusion(f32[1,4,2,256,256]{4,3,2,1,0:T(8,128)} %param.5, s32[]{:T(128)S(6)} %select_n.39, s32[]{:T(128)S(6)} %select_n.37, s32[]{:T(128)S(6)} %select_n.38), kind=kLoop, calls=%fused_computation | loop fusion | bytes 3145740 | tf_op jit(solution)/shard_map/dynamic_slice | solution.py:288
  6.0 5.2 %collective-permute-start = (f32[1,2,256,256]{3,2,1,0:T(8,128)S(1)}, f32[1,2,256,256]{3,2,1,0:T(8,128)S(1)}, u32[]{:S(2)}, u32[]{:S(2)}) collective-permute-start(f32[1,2,256,256]{3,2,1,0:T(8,128)S(1)} %get-tuple-element.43), channel_id=1, source_target_pairs={{192,0},{194,2},{196,4},{198,6},{200,8},{202,10},{204,12},{206,14}... | collective-permute-start | bytes 1572872 | tf_op jit(solution)/shard_map/ppermute | solution.py:297
  11.2 1.3 %collective-permute-start.1 = (f32[1,2,256,256]{3,2,1,0:T(8,128)S(1)}, f32[1,2,256,256]{3,2,1,0:T(8,128)S(1)}, u32[]{:S(2)}, u32[]{:S(2)}) collective-permute-start(f32[1,2,256,256]{3,2,1,0:T(8,128)S(1)} %get-tuple-element.44), channel_id=1, source_target_pairs={{128,0},{130,2},{132,4},{134,6},{136,8},{138,10},{140,12},{142,14}... | collective-permute-start | bytes 1572872 | tf_op jit(solution)/shard_map/ppermute | solution.py:297
  13.4 2.0 %collective-permute-start.7 = (f32[3,64,256]{2,1,0:T(8,128)S(1)}, f32[3,64,256]{2,1,0:T(8,128)S(1)}, u32[]{:S(2)}, u32[]{:S(2)}) collective-permute-start(f32[3,64,256]{2,1,0:T(8,128)S(1)} %constant_dynamic-update-slice_fusion.refs_9_), channel_id=1, source_target_pairs={{0,2},{1,3},{2,0},{3,1},{4,6},{5,7},{6,4},{7,5},{8,10},{9,11},{10,... | collective-permute-start | bytes 589832 | tf_op jit(solution)/shard_map/ppermute | solution.py:304
  15.6 1.6 %copy-done.1 = f32[4,2,256,256]{3,2,1,0:T(8,128)S(1)} copy-done((f32[4,2,256,256]{3,2,1,0:T(8,128)S(1)}, f32[4,2,256,256]{3,2,1,0:T(8,128)}, u32[]{:S(2)}) %copy-start.1) | copy-done | bytes 2097176
  17.3 3.6 %collective-permute-done.7.refs_11_ = f32[3,64,256]{2,1,0:T(8,128)S(1)} collective-permute-done((f32[3,64,256]{2,1,0:T(8,128)S(1)}, f32[3,64,256]{2,1,0:T(8,128)S(1)}, u32[]{:S(2)}, u32[]{:S(2)}) %collective-permute-start.7) | collective-permute-done | bytes 196640 | tf_op jit(solution)/shard_map/ppermute | solution.py:304
  20.9 1.3 %collective-permute-start.12 = (f32[1,2,256,256]{3,2,1,0:T(8,128)S(1)}, f32[1,2,256,256]{3,2,1,0:T(8,128)S(1)}, u32[]{:S(2)}, u32[]{:S(2)}) collective-permute-start(f32[1,2,256,256]{3,2,1,0:T(8,128)S(1)} %get-tuple-element.43), channel_id=1, source_target_pairs={{193,1},{195,3},{197,5},{199,7},{201,9},{203,11},{205,13},{207,15}... | collective-permute-start | bytes 1572872 | tf_op jit(solution)/shard_map/ppermute | solution.py:297
  22.3 1.3 %collective-permute-start.13 = (f32[1,2,256,256]{3,2,1,0:T(8,128)S(1)}, f32[1,2,256,256]{3,2,1,0:T(8,128)S(1)}, u32[]{:S(2)}, u32[]{:S(2)}) collective-permute-start(f32[1,2,256,256]{3,2,1,0:T(8,128)S(1)} %get-tuple-element.44), channel_id=1, source_target_pairs={{129,1},{131,3},{133,5},{135,7},{137,9},{139,11},{141,13},{143,15}... | collective-permute-start | bytes 1572872 | tf_op jit(solution)/shard_map/ppermute | solution.py:297
  23.6 5.1 %collective-permute-start.14 = (f32[1,2,256,256]{3,2,1,0:T(8,128)S(1)}, f32[1,2,256,256]{3,2,1,0:T(8,128)S(1)}, u32[]{:S(2)}, u32[]{:S(2)}) collective-permute-start(f32[1,2,256,256]{3,2,1,0:T(8,128)S(1)} %get-tuple-element.42), channel_id=1, source_target_pairs={{65,1},{67,3},{69,5},{71,7},{73,9},{75,11},{77,13},{79,15},{81,17}... | collective-permute-start | bytes 1572872 | tf_op jit(solution)/shard_map/ppermute | solution.py:297
  29.5 1.3 %collective-permute-start.10 = (f32[1,2,256,256]{3,2,1,0:T(8,128)S(1)}, f32[1,2,256,256]{3,2,1,0:T(8,128)S(1)}, u32[]{:S(2)}, u32[]{:S(2)}) collective-permute-start(f32[1,2,256,256]{3,2,1,0:T(8,128)S(1)} %get-tuple-element.26), channel_id=1, source_target_pairs={{0,128},{2,130},{4,132},{6,134},{8,136},{10,138},{12,140},{14,142}... | collective-permute-start | bytes 1572872 | tf_op jit(solution)/shard_map/ppermute | solution.py:315
  30.8 4.9 %collective-permute-done.12.refs_6_ = f32[1,2,256,256]{3,2,1,0:T(8,128)S(1)} collective-permute-done((f32[1,2,256,256]{3,2,1,0:T(8,128)S(1)}, f32[1,2,256,256]{3,2,1,0:T(8,128)S(1)}, u32[]{:S(2)}, u32[]{:S(2)}) %collective-permute-start.12) | collective-permute-done | bytes 524320 | tf_op jit(solution)/shard_map/ppermute | solution.py:297
  37.0 3.7 %collective-permute-done.13.refs_7_ = f32[1,2,256,256]{3,2,1,0:T(8,128)S(1)} collective-permute-done((f32[1,2,256,256]{3,2,1,0:T(8,128)S(1)}, f32[1,2,256,256]{3,2,1,0:T(8,128)S(1)}, u32[]{:S(2)}, u32[]{:S(2)}) %collective-permute-start.13) | collective-permute-done | bytes 524320 | tf_op jit(solution)/shard_map/ppermute | solution.py:297
  40.7 7.4 %collective-permute-done.14.refs_8_ = f32[1,2,256,256]{3,2,1,0:T(8,128)S(1)} collective-permute-done((f32[1,2,256,256]{3,2,1,0:T(8,128)S(1)}, f32[1,2,256,256]{3,2,1,0:T(8,128)S(1)}, u32[]{:S(2)}, u32[]{:S(2)}) %collective-permute-start.14) | collective-permute-done | bytes 524320 | tf_op jit(solution)/shard_map/ppermute | solution.py:297
  48.0 6.6 %chain.3 = (f32[1,2,256,256]{3,2,1,0:T(8,128)S(1)}, f32[1,2,256,256]{3,2,1,0:T(8,128)}, f32[1,2,256,256]{3,2,1,0:T(8,128)}, f32[1,2,256,256]{3,2,1,0:T(8,128)}) custom-call(s32[1]{0:T(128)} %bitcast.2.me.refs_0_, s32[1]{0:T(128)} %bitcast.refs_1_.refs_0_, s32[1]{0:T(128)} %bitcast.3.refs_2_, f32[2,256,256]{2,1,0:T(8,128)S(1)} %get-tuple-element.22.refs_3_, ...), custom_call_target="tpu_custom_call" | custom-call | flops 3221225472 | bytes 5242880 | tf_op jit(solution)/shard_map/chain/pallas_call | solution.py:113
  54.6 1.9 %collective-permute-start.15 = (f32[1,2,256,256]{3,2,1,0:T(8,128)}, f32[1,2,256,256]{3,2,1,0:T(8,128)S(1)}, u32[]{:S(2)}, u32[]{:S(2)}) collective-permute-start(f32[1,2,256,256]{3,2,1,0:T(8,128)} %get-tuple-element.33), channel_id=1, source_target_pairs={{1,65},{3,67},{5,69},{7,71},{9,73},{11,75},{13,77},{15,79},{17,81}... | collective-permute-start | bytes 1572872 | tf_op jit(solution)/shard_map/ppermute | solution.py:315
  56.5 2.1 %collective-permute-start.16 = (f32[1,2,256,256]{3,2,1,0:T(8,128)}, f32[1,2,256,256]{3,2,1,0:T(8,128)}, u32[]{:S(2)}, u32[]{:S(2)}) collective-permute-start(f32[1,2,256,256]{3,2,1,0:T(8,128)} %get-tuple-element.34), channel_id=1, source_target_pairs={{1,129},{3,131},{5,133},{7,135},{9,137},{11,139},{13,141},{15,143}... | collective-permute-start | bytes 1572872 | tf_op jit(solution)/shard_map/ppermute | solution.py:315
  58.7 4.7 %collective-permute-start.17 = (f32[1,2,256,256]{3,2,1,0:T(8,128)}, f32[1,2,256,256]{3,2,1,0:T(8,128)}, u32[]{:S(2)}, u32[]{:S(2)}) collective-permute-start(f32[1,2,256,256]{3,2,1,0:T(8,128)} %get-tuple-element.35), channel_id=1, source_target_pairs={{1,193},{3,195},{5,197},{7,199},{9,201},{11,203},{13,205},{15,207}... | collective-permute-start | bytes 1572872 | tf_op jit(solution)/shard_map/ppermute | solution.py:315
  63.5 1.9 %collective-permute-start.19 = (f32[2,2,256,256]{3,2,1,0:T(8,128)S(1)}, f32[2,2,256,256]{3,2,1,0:T(8,128)S(1)}, u32[]{:S(2)}, u32[]{:S(2)}) collective-permute-start(f32[2,2,256,256]{3,2,1,0:T(8,128)S(1)} %pack.2.refs_2_), channel_id=1, source_target_pairs={{1,2},{2,1},{3,4},{4,3},{5,6},{6,5},{7,8},{8,7},{9,10},{10,9},{11,... | collective-permute-start | bytes 3145736 | tf_op jit(solution)/shard_map/ppermute | solution.py:325
  65.9 4.6 %collective-permute-done.17.refs_5_ = f32[1,2,256,256]{3,2,1,0:T(8,128)} collective-permute-done((f32[1,2,256,256]{3,2,1,0:T(8,128)}, f32[1,2,256,256]{3,2,1,0:T(8,128)}, u32[]{:S(2)}, u32[]{:S(2)}) %collective-permute-start.17) | collective-permute-done | bytes 524320 | tf_op jit(solution)/shard_map/ppermute | solution.py:315
  70.5 1.3 %pack.3.refs_3_ = f32[2,2,256,256]{3,2,1,0:T(8,128)S(1)} custom-call(s32[1]{0:T(128)} %bitcast.2.me.refs_0_, s32[1]{0:T(128)} %bitcast.refs_1_.refs_0_, f32[1,2,256,256]{3,2,1,0:T(8,128)S(1)} %get-tuple-element.36.refs_2_, f32[1,2,256,256]{3,2,1,0:T(8,128)S(1)} %collective-permute-done.15.refs_3_, f32[1,2,256,256]{3,2,1,0:T(8,128)} %collective-permute-done.16.refs_4_, ...), custom_call_target="tpu_custom_call" | custom-call | tf_op jit(solution)/shard_map/pack/pallas_call | solution.py:150
  72.1 1.9 %band_own.1 = (f32[4,2,256,256]{3,2,1,0:T(8,128)}, f32[4,2,256,256]{3,2,1,0:T(8,128)S(1)}) custom-call(s32[1]{0:T(128)} %bitcast.refs_1_.refs_0_, f32[4,8]{1,0:T(4,128)S(1)} %select_reduce_fusion.refs_1_, f32[2,2,256,256]{3,2,1,0:T(8,128)S(1)} %pack.2.refs_2_, f32[2,2,256,256]{3,2,1,0:T(8,128)S(1)} %pack.3.refs_3_), custom_call_target="tpu_custom_call" | custom-call | tf_op jit(solution)/shard_map/band_own/pallas_call | solution.py:194
  74.0 7.7 %collective-permute-done.19.value = f32[2,2,256,256]{3,2,1,0:T(8,128)S(1)} collective-permute-done((f32[2,2,256,256]{3,2,1,0:T(8,128)S(1)}, f32[2,2,256,256]{3,2,1,0:T(8,128)S(1)}, u32[]{:S(2)}, u32[]{:S(2)}) %collective-permute-start.19) | collective-permute-done | bytes 1048608 | tf_op jit(solution)/shard_map/ppermute | solution.py:325
  81.8 2.1 %band_halo.1 = f32[4,2,256,256]{3,2,1,0:T(8,128)} custom-call(s32[1]{0:T(128)} %bitcast.refs_1_.refs_0_, f32[4,8]{1,0:T(4,128)S(1)} %select_reduce_fusion.refs_1_, f32[4,2,256,256]{3,2,1,0:T(8,128)S(1)} %get-tuple-element.41.refs_2_, f32[2,2,256,256]{3,2,1,0:T(8,128)S(1)} %collective-permute-done.18.refs_3_, f32[2,2,256,256]{3,2,1,0:T(8,128)S(1)} %admit.1.refs_4_), custom_call_target="tpu_custom_call" | custom-call | tf_op jit(solution)/shard_map/band_halo/pallas_call | solution.py:248
  (45 shorter events, 5.6 us)
Async XLA Ops:
  0.6 15.0 %copy-start = (f32[1,4,2,256,256]{4,3,2,1,0:T(8,128)S(1)}, f32[1,4,2,256,256]{4,3,2,1,0:T(8,128)}, u32[]{:S(2)}) copy-start(f32[1,4,2,256,256]{4,3,2,1,0:T(8,128)} %param.5) | copy-start | bytes 6291460
  1.7 10.9 %collective-permute-start.3 = (f32[1,64,256]{2,1,0:T(8,128)S(1)}, f32[1,64,256]{2,1,0:T(8,128)S(1)}, u32[]{:S(2)}, u32[]{:S(2)}) collective-permute-start(f32[1,64,256]{2,1,0:T(8,128)S(1)} %constant_dynamic-slice_fusion), channel_id=1, source_target_pairs={{0,64},{64,128},{128,192},{192,0},{1,65},{65,129},{129,193},{193,1... | collective-permute-start | bytes 196616 | tf_op jit(solution)/shard_map/ppermute | solution.py:273
  2.1 11.1 %collective-permute-start.4 = (f32[1,64,256]{2,1,0:T(8,128)S(1)}, f32[1,64,256]{2,1,0:T(8,128)S(1)}, u32[]{:S(2)}, u32[]{:S(2)}) collective-permute-start(f32[1,64,256]{2,1,0:T(8,128)S(1)} %constant_dynamic-slice_fusion), channel_id=1, source_target_pairs={{0,128},{64,192},{128,0},{192,64},{1,129},{65,193},{129,1},{193,65... | collective-permute-start | bytes 196616 | tf_op jit(solution)/shard_map/ppermute | solution.py:273
  4.6 8.7 %collective-permute-start.5 = (f32[1,64,256]{2,1,0:T(8,128)S(1)}, f32[1,64,256]{2,1,0:T(8,128)S(1)}, u32[]{:S(2)}, u32[]{:S(2)}) collective-permute-start(f32[1,64,256]{2,1,0:T(8,128)S(1)} %constant_dynamic-slice_fusion), channel_id=1, source_target_pairs={{0,192},{64,0},{128,64},{192,128},{1,193},{65,1},{129,65},{193,129... | collective-permute-start | bytes 196616 | tf_op jit(solution)/shard_map/ppermute | solution.py:273
  6.0 17.6 %collective-permute-start = (f32[1,2,256,256]{3,2,1,0:T(8,128)S(1)}, f32[1,2,256,256]{3,2,1,0:T(8,128)S(1)}, u32[]{:S(2)}, u32[]{:S(2)}) collective-permute-start(f32[1,2,256,256]{3,2,1,0:T(8,128)S(1)} %get-tuple-element.43), channel_id=1, source_target_pairs={{192,0},{194,2},{196,4},{198,6},{200,8},{202,10},{204,12},{206,14}... | collective-permute-start | bytes 1572872 | tf_op jit(solution)/shard_map/ppermute | solution.py:297
  11.2 17.5 %collective-permute-start.1 = (f32[1,2,256,256]{3,2,1,0:T(8,128)S(1)}, f32[1,2,256,256]{3,2,1,0:T(8,128)S(1)}, u32[]{:S(2)}, u32[]{:S(2)}) collective-permute-start(f32[1,2,256,256]{3,2,1,0:T(8,128)S(1)} %get-tuple-element.44), channel_id=1, source_target_pairs={{128,0},{130,2},{132,4},{134,6},{136,8},{138,10},{140,12},{142,14}... | collective-permute-start | bytes 1572872 | tf_op jit(solution)/shard_map/ppermute | solution.py:297
  12.5 16.2 %collective-permute-start.2 = (f32[1,2,256,256]{3,2,1,0:T(8,128)S(1)}, f32[1,2,256,256]{3,2,1,0:T(8,128)S(1)}, u32[]{:S(2)}, u32[]{:S(2)}) collective-permute-start(f32[1,2,256,256]{3,2,1,0:T(8,128)S(1)} %get-tuple-element.42), channel_id=1, source_target_pairs={{64,0},{66,2},{68,4},{70,6},{72,8},{74,10},{76,12},{78,14},{80,16}... | collective-permute-start | bytes 1572872 | tf_op jit(solution)/shard_map/ppermute | solution.py:297
  13.3 2.1 %collective-permute-start.6 = (f32[3,64,256]{2,1,0:T(8,128)S(1)}, f32[3,64,256]{2,1,0:T(8,128)S(1)}, u32[]{:S(2)}, u32[]{:S(2)}) collective-permute-start(f32[3,64,256]{2,1,0:T(8,128)S(1)} %constant_dynamic-update-slice_fusion.refs_9_), channel_id=1, source_target_pairs={{0,1},{1,0},{2,3},{3,2},{4,5},{5,4},{6,7},{7,6},{8,9},{9,8},{10,11... | collective-permute-start | bytes 589832 | tf_op jit(solution)/shard_map/ppermute | solution.py:304
  13.4 7.5 %collective-permute-start.7 = (f32[3,64,256]{2,1,0:T(8,128)S(1)}, f32[3,64,256]{2,1,0:T(8,128)S(1)}, u32[]{:S(2)}, u32[]{:S(2)}) collective-permute-start(f32[3,64,256]{2,1,0:T(8,128)S(1)} %constant_dynamic-update-slice_fusion.refs_9_), channel_id=1, source_target_pairs={{0,2},{1,3},{2,0},{3,1},{4,6},{5,7},{6,4},{7,5},{8,10},{9,11},{10,... | collective-permute-start | bytes 589832 | tf_op jit(solution)/shard_map/ppermute | solution.py:304
  15.4 6.9 %collective-permute-start.8 = (f32[3,64,256]{2,1,0:T(8,128)S(1)}, f32[3,64,256]{2,1,0:T(8,128)S(1)}, u32[]{:S(2)}, u32[]{:S(2)}) collective-permute-start(f32[3,64,256]{2,1,0:T(8,128)S(1)} %constant_dynamic-update-slice_fusion.refs_9_), channel_id=1, source_target_pairs={{0,17},{1,16},{2,19},{3,18},{4,21},{5,20},{6,23},{7,22},{8,25},{9,... | collective-permute-start | bytes 589832 | tf_op jit(solution)/shard_map/ppermute | solution.py:304
  17.2 11.5 %copy-start.2 = (f32[1,256,256]{2,1,0:T(8,128)S(1)}, f32[1,256,256]{2,1,0:T(8,128)}, u32[]{:S(2)}) copy-start(f32[1,256,256]{2,1,0:T(8,128)} %refs_5_.3) | copy-start | bytes 786436
  20.9 14.8 %collective-permute-start.12 = (f32[1,2,256,256]{3,2,1,0:T(8,128)S(1)}, f32[1,2,256,256]{3,2,1,0:T(8,128)S(1)}, u32[]{:S(2)}, u32[]{:S(2)}) collective-permute-start(f32[1,2,256,256]{3,2,1,0:T(8,128)S(1)} %get-tuple-element.43), channel_id=1, source_target_pairs={{193,1},{195,3},{197,5},{199,7},{201,9},{203,11},{205,13},{207,15}... | collective-permute-start | bytes 1572872 | tf_op jit(solution)/shard_map/ppermute | solution.py:297
  22.3 18.4 %collective-permute-start.13 = (f32[1,2,256,256]{3,2,1,0:T(8,128)S(1)}, f32[1,2,256,256]{3,2,1,0:T(8,128)S(1)}, u32[]{:S(2)}, u32[]{:S(2)}) collective-permute-start(f32[1,2,256,256]{3,2,1,0:T(8,128)S(1)} %get-tuple-element.44), channel_id=1, source_target_pairs={{129,1},{131,3},{133,5},{135,7},{137,9},{139,11},{141,13},{143,15}... | collective-permute-start | bytes 1572872 | tf_op jit(solution)/shard_map/ppermute | solution.py:297
  23.6 24.4 %collective-permute-start.14 = (f32[1,2,256,256]{3,2,1,0:T(8,128)S(1)}, f32[1,2,256,256]{3,2,1,0:T(8,128)S(1)}, u32[]{:S(2)}, u32[]{:S(2)}) collective-permute-start(f32[1,2,256,256]{3,2,1,0:T(8,128)S(1)} %get-tuple-element.42), channel_id=1, source_target_pairs={{65,1},{67,3},{69,5},{71,7},{73,9},{75,11},{77,13},{79,15},{81,17}... | collective-permute-start | bytes 1572872 | tf_op jit(solution)/shard_map/ppermute | solution.py:297
  28.8 29.9 %collective-permute-start.9 = (f32[1,2,256,256]{3,2,1,0:T(8,128)S(1)}, f32[1,2,256,256]{3,2,1,0:T(8,128)S(1)}, u32[]{:S(2)}, u32[]{:S(2)}) collective-permute-start(f32[1,2,256,256]{3,2,1,0:T(8,128)S(1)} %get-tuple-element.25), channel_id=1, source_target_pairs={{0,64},{2,66},{4,68},{6,70},{8,72},{10,74},{12,76},{14,78},{16,80}... | collective-permute-start | bytes 1572872 | tf_op jit(solution)/shard_map/ppermute | solution.py:315
  29.5 33.9 %collective-permute-start.10 = (f32[1,2,256,256]{3,2,1,0:T(8,128)S(1)}, f32[1,2,256,256]{3,2,1,0:T(8,128)S(1)}, u32[]{:S(2)}, u32[]{:S(2)}) collective-permute-start(f32[1,2,256,256]{3,2,1,0:T(8,128)S(1)} %get-tuple-element.26), channel_id=1, source_target_pairs={{0,128},{2,130},{4,132},{6,134},{8,136},{10,138},{12,140},{14,142}... | collective-permute-start | bytes 1572872 | tf_op jit(solution)/shard_map/ppermute | solution.py:315
  35.7 27.7 %collective-permute-start.11 = (f32[1,2,256,256]{3,2,1,0:T(8,128)S(1)}, f32[1,2,256,256]{3,2,1,0:T(8,128)S(1)}, u32[]{:S(2)}, u32[]{:S(2)}) collective-permute-start(f32[1,2,256,256]{3,2,1,0:T(8,128)S(1)} %get-tuple-element.27), channel_id=1, source_target_pairs={{0,192},{2,194},{4,196},{6,198},{8,200},{10,202},{12,204},{14,206}... | collective-permute-start | bytes 1572872 | tf_op jit(solution)/shard_map/ppermute | solution.py:315
  54.6 11.3 %collective-permute-start.15 = (f32[1,2,256,256]{3,2,1,0:T(8,128)}, f32[1,2,256,256]{3,2,1,0:T(8,128)S(1)}, u32[]{:S(2)}, u32[]{:S(2)}) collective-permute-start(f32[1,2,256,256]{3,2,1,0:T(8,128)} %get-tuple-element.33), channel_id=1, source_target_pairs={{1,65},{3,67},{5,69},{7,71},{9,73},{11,75},{13,77},{15,79},{17,81}... | collective-permute-start | bytes 1572872 | tf_op jit(solution)/shard_map/ppermute | solution.py:315
  56.5 9.4 %collective-permute-start.16 = (f32[1,2,256,256]{3,2,1,0:T(8,128)}, f32[1,2,256,256]{3,2,1,0:T(8,128)}, u32[]{:S(2)}, u32[]{:S(2)}) collective-permute-start(f32[1,2,256,256]{3,2,1,0:T(8,128)} %get-tuple-element.34), channel_id=1, source_target_pairs={{1,129},{3,131},{5,133},{7,135},{9,137},{11,139},{13,141},{15,143}... | collective-permute-start | bytes 1572872 | tf_op jit(solution)/shard_map/ppermute | solution.py:315
  58.7 11.8 %collective-permute-start.17 = (f32[1,2,256,256]{3,2,1,0:T(8,128)}, f32[1,2,256,256]{3,2,1,0:T(8,128)}, u32[]{:S(2)}, u32[]{:S(2)}) collective-permute-start(f32[1,2,256,256]{3,2,1,0:T(8,128)} %get-tuple-element.35), channel_id=1, source_target_pairs={{1,193},{3,195},{5,197},{7,199},{9,201},{11,203},{13,205},{15,207}... | collective-permute-start | bytes 1572872 | tf_op jit(solution)/shard_map/ppermute | solution.py:315
  63.5 8.5 %copy-start.3 = (f32[1,6]{1,0:T(1,128)S(1)}, f32[1,6]{1,0:T(1,128)}, u32[]{:S(2)}) copy-start(f32[1,6]{1,0:T(1,128)} %param.9) | copy-start | bytes 76
  63.5 8.5 %copy-start.4 = (s32[6]{0:T(128)S(1)}, s32[6]{0:T(128)}, u32[]{:S(2)}) copy-start(s32[6]{0:T(128)} %param.8) | copy-start | bytes 76
  63.5 18.2 %collective-permute-start.19 = (f32[2,2,256,256]{3,2,1,0:T(8,128)S(1)}, f32[2,2,256,256]{3,2,1,0:T(8,128)S(1)}, u32[]{:S(2)}, u32[]{:S(2)}) collective-permute-start(f32[2,2,256,256]{3,2,1,0:T(8,128)S(1)} %pack.2.refs_2_), channel_id=1, source_target_pairs={{1,2},{2,1},{3,4},{4,3},{5,6},{6,5},{7,8},{8,7},{9,10},{10,9},{11,... | collective-permute-start | bytes 3145736 | tf_op jit(solution)/shard_map/ppermute | solution.py:325
  71.8 10.0 %collective-permute-start.18 = (f32[2,2,256,256]{3,2,1,0:T(8,128)S(1)}, f32[2,2,256,256]{3,2,1,0:T(8,128)S(1)}, u32[]{:S(2)}, u32[]{:S(2)}) collective-permute-start(f32[2,2,256,256]{3,2,1,0:T(8,128)S(1)} %pack.3.refs_3_), channel_id=1, source_target_pairs={{0,1},{1,0},{2,3},{3,2},{4,5},{5,4},{6,7},{7,6},{8,9},{9,8},{10,11... | collective-permute-start | bytes 3145736 | tf_op jit(solution)/shard_map/ppermute | solution.py:326
  (1 other events, 1.6 us)
where the time goes:
time: 84.5 us; the launch traced here: 84.1 us
  starting transfers between devices  34.1 us (40%)
  waiting for transfers between devices  32.4 us (38%)
  Pallas kernels  12.1 us (14%)
  local copies, waits for them, and re-layouts  4.08 us (5%)
  between operations  1.14 us (1%)
    ppermute x6, waiting for transfers between devices, on_device(): lax.ppermute(value, both, batch_pairs(batch, shift, True))  16 us
    ppermute x6, starting transfers between devices, on_device(): lax.ppermute(value, both, batch_pairs(batch, shift, True))  14.9 us
    ppermute x6, starting transfers between devices, on_device(): lax.ppermute(produced[shift], both, batch_pairs(batch, shift, False))  12 us
    ppermute x1, waiting for transfers between devices, on_device(): far_halo = lax.ppermute(packed[0], 'en', across)  7.72 us
    pallas_call x2, Pallas kernels, run_chain(): pl.pallas_call(lambda *refs: chain_kernel(batch, parts, *refs), out_shape...  6.62 us
    ppermute x6, waiting for transfers between devices, on_device(): lax.ppermute(produced[shift], both, batch_pairs(batch, shift, False))  5.05 us
    ppermute x3, waiting for transfers between devices, on_device(): lax.ppermute(first, 'en', [(source, source ^ partner) for source in range...  3.69 us
    ppermute x3, starting transfers between devices, ring(): return lax.ppermute(value, 'sec', pairs)  2.9 us
  transfers between devices with their start and end apart: 20, of which 8 were waited for; matrix products, arithmetic and copies ran while one was open for 2% of the time, Pallas kernels for 12%

commit v1 on v0

v1 whole, which is shorter than its diff:
```python
import jax
import jax.numpy as jnp
from jax import lax
from jax.experimental import pallas as pl
from jax.experimental.pallas import tpu as pltpu
from jax.sharding import PartitionSpec as P

F32 = jnp.float32
BF16 = jnp.bfloat16
NN = (((1,), (0,)), ((), ()))
NT = (((1,), (1,)), ((), ()))
VMEM = pl.BlockSpec(memory_space=pltpu.VMEM)
SMEM = pl.BlockSpec(memory_space=pltpu.SMEM)
HBM = pl.BlockSpec(memory_space=pltpu.HBM)
PARAMS = pltpu.CompilerParams(vmem_limit_bytes=36 * 1024 * 1024)
EARLY = (0, 1, 3)
ROWS = 32
LATE = 2
SMALL = pltpu.CompilerParams(vmem_limit_bytes=8 * 1024 * 1024)
def split(value):
    high = value.astype(BF16)
    return high, (value - high.astype(F32)).astype(BF16)


def dot3(left, right, dims):
    def one(a, b):
        return lax.dot_general(a, b, dims, preferred_element_type=F32)

    return one(left[0], right[0]) + (one(left[0], right[1]) + one(left[1], right[0]))


def triple(real, imag):
    return split(real), split(imag), split(real + imag)


def gauss(left, right, dims):
    first, second, third = (dot3(a, b, dims) for a, b in zip(left, right))
    return first - second, third - first - second


def store_transfer(inverse, coupling, high, low, stage):
    orb = coupling.shape[-1]
    both = dot3(split(inverse.reshape(2 * orb, orb)), split(coupling), NN)
    for number, (upper, lower) in enumerate(triple(both[:orb], both[orb:])):
        high[stage, number] = upper
        low[stage, number] = lower


def pick_kernel(me, inverse_all, boundary_all, kept, start, sems):
    copies = [
        pltpu.make_async_copy(inverse_all.at[me[0]], kept, sems.at[0]),
        pltpu.make_async_copy(boundary_all.at[me[0]], start, sems.at[1]),
    ]
    for copy in copies:
        copy.start()
    for copy in copies:
        copy.wait()


def run_pick(me, inverse_blocks, boundary):
    block = jax.ShapeDtypeStruct(inverse_blocks.shape[1:], F32)
    return pl.pallas_call(
        pick_kernel,
        out_shape=[block] * 2,
        in_specs=[SMEM] + [HBM] * 2,
        out_specs=[VMEM] * 2,
        scratch_shapes=[pltpu.SemaphoreType.DMA((2,))],
        compiler_params=SMALL,
        name="pick",
    )(me, inverse_blocks, boundary)


def chain_kernel(parts, me_ref, quarter_ref, kept, start, own_coupling, *refs):
    arrived = refs[: parts - 1]
    quarters = refs[parts - 1 : 2 * parts - 1]
    outs = refs[2 * parts - 1 : 3 * parts]
    high, low, inverse, previous, coupling = refs[3 * parts :]
    me = me_ref[0]
    orb = coupling.shape[-1]
    rows = orb // len(quarters)

    coupling[0] = own_coupling[0]
    for number, source in enumerate(quarters):
        quarter = lax.bitwise_xor(quarter_ref[0], number)
        place = pl.ds(pl.multiple_of(quarter * rows, rows), rows)
        for shift in range(1, parts):
            coupling[shift, place, :] = source[shift - 1]
    for shift in range(parts):
        stage = lax.rem(me - shift + parts, parts)
        inverse[stage] = kept[...] if shift == 0 else arrived[shift - 1][0]
        store_transfer(inverse[stage], coupling[shift], high, low, stage)
    previous[...] = start[...]
    for stage in range(parts):
        transfer = [(high[stage, number], low[stage, number]) for number in range(3)]
        half = gauss(transfer, triple(previous[0], previous[1]), NN)
        real, imag = gauss(triple(*half), transfer, NT)
        real = real + inverse[stage, 0]
        imag = imag + inverse[stage, 1]
        if stage < parts - 1:
            previous[0] = real
            previous[1] = imag
        target = lax.rem(stage - me + parts, parts)
        for number in range(parts):

            @pl.when(target == number)
            def _():
                outs[number][0, 0] = real
                if number == LATE:
                    outs[parts][0, 0] = imag
                else:
                    outs[number][0, 1] = imag


def run_chain(me, quarter, kept, start, coupling, arrived, quarters):
    parts = len(arrived) + 1
    orb = start.shape[-1]
    outs = [jax.ShapeDtypeStruct((1, 2, orb, orb), F32)] * parts
    outs[LATE] = jax.ShapeDtypeStruct((1, 1, orb, orb), F32)
    outs.append(outs[LATE])
    return pl.pallas_call(
        lambda *refs: chain_kernel(parts, *refs),
        out_shape=outs,
        in_specs=[SMEM] * 2 + [VMEM] * (3 + len(arrived) + len(quarters)),
        out_specs=[VMEM] * (parts + 1),
        scratch_shapes=[
            pltpu.VMEM((parts, 3, orb, orb), BF16),
            pltpu.VMEM((parts, 3, orb, orb), BF16),
            pltpu.VMEM((parts, 2, orb, orb), F32),
            pltpu.VMEM((2, orb, orb), F32),
            pltpu.VMEM((parts, orb, orb), F32),
        ],
        compiler_params=PARAMS,
        cost_estimate=pl.CostEstimate(
            flops=parts * 48 * orb**3,
            bytes_accessed=parts * 20 * orb * orb,
            transcendentals=0,
        ),
        name="chain",
    )(me, quarter, kept, start, coupling, *arrived, *quarters)


def mix(weights, columns, values, row):
    total = weights[row, columns[0]] * values[0]
    for column, value in zip(columns[1:], values[1:]):
        total = total + weights[row, column] * value
    return total


def early_kernel(count, scalars, weights, *refs):
    slots = refs[: 2 * len(EARLY)]
    green, partial, sems = refs[2 * len(EARLY) :]
    me = scalars[0]
    orb = partial.shape[-1]
    copies = []
    for number, shift in enumerate(EARLY):
        place = lax.rem(me - shift + count, count)
        copies.append(pltpu.make_async_copy(slots[number].at[0], green.at[place], sems.at[number]))
    for copy in copies:
        copy.start()
    columns = list(EARLY) + [count + shift for shift in EARLY]
    rows = 32
    for half in range(2):

        @pl.loop(0, orb // rows)
        def _(step):
            place = pl.ds(pl.multiple_of(step * rows, rows), rows)
            values = [slot[0, half, place, :] for slot in slots]
            for row in range(count):
                partial[half, row, place, :] = mix(weights, columns, values, row)

    for copy in copies:
        copy.wait()


def run_early(me, weights, slots):
    count = weights.shape[0]
    orb = slots[0].shape[-1]
    return pl.pallas_call(
        lambda *refs: early_kernel(count, *refs),
        out_shape=[
            jax.ShapeDtypeStruct((count, 2, orb, orb), F32),
            jax.ShapeDtypeStruct((2, count, orb, orb), F32),
        ],
        in_specs=[SMEM, SMEM] + [VMEM] * len(slots),
        out_specs=[HBM, VMEM],
        scratch_shapes=[pltpu.SemaphoreType.DMA((len(EARLY),))],
        compiler_params=SMALL,
        cost_estimate=pl.CostEstimate(
            flops=0, bytes_accessed=64 * orb * orb, transcendentals=0
        ),
        name="band_early",
    )(me[None], weights, *slots)


def late_kernel(count, me_ref, weights, partial, *refs):
    slots, halos = refs[:2], refs[2:4]
    green, energy, done, sems = refs[5:]
    orb = partial.shape[-1]
    place = lax.rem(me_ref[0] - LATE + count, count)
    copies = []
    for half, slot in enumerate(slots):
        copies.append(pltpu.make_async_copy(slot.at[0, 0], green.at[place, half], sems.at[half]))
        copies[-1].start()
    for row in range(count):
        for half in range(2):

            @pl.loop(0, orb // ROWS)
            def _(step):
                where = pl.ds(pl.multiple_of(step * ROWS, ROWS), ROWS)
                values = [slots[half][0, 0, where, :], halos[half][0, 0, where, :]]
                done[row, half, where, :] = partial[half, row, where, :] + mix(
                    weights, (LATE, count + LATE), values, row
                )

        copy = pltpu.make_async_copy(done.at[row], energy.at[row], sems.at[2 + row])
        copy.start()
        copies.append(copy)
    for copy in copies:
        copy.wait()


def run_late(me, weights, partial, slots, halos, green):
    count = weights.shape[0]
    whole = jax.ShapeDtypeStruct(green.shape, F32)
    return pl.pallas_call(
        lambda *refs: late_kernel(count, *refs),
        out_shape=[whole] * 2,
        in_specs=[SMEM, SMEM] + [VMEM] * 5 + [HBM],
        out_specs=[HBM] * 2,
        input_output_aliases={7: 0},
        scratch_shapes=[pltpu.VMEM(green.shape, F32), pltpu.SemaphoreType.DMA((2 + count,))],
        compiler_params=SMALL,
        name="band_late",
    )(me[None], weights, partial, *slots, *halos, green)


def admit_kernel(value, kept):
    pass


def run_admit(value):
    return pl.pallas_call(
        admit_kernel,
        out_shape=jax.ShapeDtypeStruct(value.shape, F32),
        in_specs=[VMEM],
        out_specs=VMEM,
        input_output_aliases={0: 0},
        compiler_params=SMALL,
        cost_estimate=pl.CostEstimate(flops=1_000_000_000, bytes_accessed=0, transcendentals=0),
        name="admit",
    )(value)


def on_device(inverse_blocks, coupling, boundary, band_offsets, band_weights):
    parts, devices = lax.axis_size("sec"), lax.axis_size("en")
    own_inverse = inverse_blocks[0]
    count = own_inverse.shape[0]
    me, lane = lax.axis_index("sec"), lax.axis_index("en")
    orb = coupling.shape[-1]
    rows = orb // 4
    core = lax.rem(lane, 2)
    quarter = core + 2 * lax.rem(lane // 2 + lane // 16, 2)
    both = ("sec", "en")

    def ring(value, shift):
        pairs = [(source, (source + shift) % parts) for source in range(parts)]
        return lax.ppermute(value, "sec", pairs)

    def halo(value, shift):
        pairs = []
        for sec in range(parts):
            step = 1 if (sec - shift) % parts >= count // 2 else -1
            for en in range(devices):
                if 0 <= en + step < devices:
                    pairs.append((sec * devices + en, sec * devices + en + step))
        return lax.ppermute(value, both, pairs)

    def after(values, *waits):
        return list(lax.optimization_barrier((tuple(values), waits))[0])

    sent = [
        lax.dynamic_slice_in_dim(own_inverse, lax.rem(me + shift, parts), 1, axis=0)
        for shift in range(1, parts)
    ]
    piece = lax.dynamic_slice(coupling, (0, quarter * rows, 0), (1, rows, orb))
    piece = after([piece], *sent)[0]
    gathered = [ring(piece, shift) for shift in range(1, parts)]
    arrived = [ring(value, shift) for shift, value in enumerate(sent, 1)]
    first = jnp.concatenate(gathered, axis=0)
    partners = (0, 1, 2, 17)
    quarters = [first] + [
        lax.ppermute(first, "en", [(source, source ^ partner) for source in range(devices)])
        for partner in partners[1:]
    ]
    kept, start = run_pick(me[None], own_inverse, boundary)

    produced = run_chain(me[None], quarter[None], kept, start, coupling, arrived, quarters)
    early = [produced[0]] + [ring(produced[shift], shift) for shift in EARLY[1:]]
    halos = [halo(early[0], 0)]
    early[1:] = [run_admit(value) for value in early[1:]]
    late = after([produced[LATE], produced[parts]], *early[1:], *halos)
    late = [ring(value, LATE) for value in late]
    halos += [halo(value, shift) for shift, value in zip(EARLY[1:], early[1:])]
    late_halos = [halo(value, LATE) for value in late]

    local = lax.rem(me - jnp.arange(parts, dtype=jnp.int32) + parts, parts)
    beyond = jnp.where(local >= count // 2, local - count, local + count)
    place = jnp.concatenate([local, beyond])
    away = place[None, :] - jnp.arange(count, dtype=jnp.int32)[:, None]
    hits = (band_offsets[:, None, None] == away[None]).astype(F32)
    weights = jnp.sum(band_weights[0][:, None, None] * hits, axis=0)
    green, partial = run_early(me, weights, early + halos)
    green, energy = run_late(me, weights, partial, late, late_halos, green)
    return green[None], energy[None]


def solution(mesh):
    return jax.shard_map(
        on_device,
        mesh=mesh,
        in_specs=(
            P("sec", "en", None, None, None),
            P("sec", None, None),
            P("en", None, None, None),
            P(),
            P("sec", None),
        ),
        out_specs=(P("sec", "en", None, None, None), P("sec", "en", None, None, None)),
        check_vma=False,
    )
```

time: 84.5 us -> 82.9 us (0.981)
  the two profiles are of different devices: /device:TPU:14 before, /device:TPU:26 now
where the time goes in v1:
time: 82.9 us; the launch traced here: 82.6 us
  waiting for transfers between devices  34.5 us (42%)
  starting transfers between devices  33.7 us (41%)
  Pallas kernels  9.18 us (11%)
  local copies, waits for them, and re-layouts  4.14 us (5%)
  between operations  0.87 us (1%)
    ppermute x10, waiting for transfers between devices, ring(): return lax.ppermute(value, 'sec', pairs)  19.5 us
    ppermute x5, starting transfers between devices, halo(): return lax.ppermute(value, both, pairs)  16.8 us
    ppermute x10, starting transfers between devices, ring(): return lax.ppermute(value, 'sec', pairs)  14.8 us
    ppermute x5, waiting for transfers between devices, halo(): return lax.ppermute(value, both, pairs)  10.5 us
    pallas_call x1, Pallas kernels, run_chain(): pl.pallas_call(lambda *refs: chain_kernel(parts, *refs), out_shape=outs,...  5.23 us
    ppermute x3, waiting for transfers between devices, on_device(): lax.ppermute(first, 'en', [(source, source ^ partner) for source in range...  4.49 us
    pallas_call x1, Pallas kernels, run_late(): pl.pallas_call(lambda *refs: late_kernel(count, *refs), out_shape=[whole]...  2.12 us
    ppermute x3, starting transfers between devices, on_device(): lax.ppermute(first, 'en', [(source, source ^ partner) for source in range...  2.1 us
  transfers between devices with their start and end apart: 18, of which 11 were waited for; matrix products, arithmetic and copies ran while one was open for 0% of the time, Pallas kernels for 2%

profile of v1, /device:TPU:26, one launch (start us, length us, event | category | flops | bytes accessed | tf_op | source)
XLA Modules:
  0.0 82.6 jit_solution(275993833815807947)
XLA Ops:
  1.7 1.5 %dynamic-slice_bitcast_fusion = (f32[1,2,256,256]{3,2,1,0:T(8,128)S(1)}, f32[1,2,256,256]{3,2,1,0:T(8,128)S(1)}, f32[1,2,256,256]{3,2,1,0:T(8,128)S(1)}) fusion(f32[1,4,2,256,256]{4,3,2,1,0:T(8,128)} %param.5, s32[]{:T(128)S(6)} %select_n.29, s32[]{:T(128)S(6)} %select_n.27, s32[]{:T(128)S(6)} %select_n.28), kind=kLoop, calls=%fused_computation | loop fusion | bytes 3145740 | tf_op jit(solution)/shard_map/dynamic_slice | solution.py:282
  3.2 1.6 %collective-permute-start.3 = (f32[1,64,256]{2,1,0:T(8,128)S(1)}, f32[1,64,256]{2,1,0:T(8,128)S(1)}, u32[]{:S(2)}, u32[]{:S(2)}) collective-permute-start(f32[1,64,256]{2,1,0:T(8,128)S(1)} %constant_dynamic-slice_fusion), channel_id=1, source_target_pairs={{0,64},{64,128},{128,192},{192,0},{1,65},{65,129},{129,193},{193,1... | collective-permute-start | bytes 196616 | tf_op jit(solution)/shard_map/ppermute | solution.py:267
  5.3 2.1 %collective-permute-start.4 = (f32[1,64,256]{2,1,0:T(8,128)S(1)}, f32[1,64,256]{2,1,0:T(8,128)S(1)}, u32[]{:S(2)}, u32[]{:S(2)}) collective-permute-start(f32[1,64,256]{2,1,0:T(8,128)S(1)} %constant_dynamic-slice_fusion), channel_id=1, source_target_pairs={{0,128},{64,192},{128,0},{192,64},{1,129},{65,193},{129,1},{193,65... | collective-permute-start | bytes 196616 | tf_op jit(solution)/shard_map/ppermute | solution.py:267
  7.4 1.4 %collective-permute-start.2 = (f32[1,2,256,256]{3,2,1,0:T(8,128)S(1)}, f32[1,2,256,256]{3,2,1,0:T(8,128)S(1)}, u32[]{:S(2)}, u32[]{:S(2)}) collective-permute-start(f32[1,2,256,256]{3,2,1,0:T(8,128)S(1)} %get-tuple-element.30), channel_id=1, source_target_pairs={{0,192},{64,0},{128,64},{192,128},{1,193},{65,1},{129,65},{193,129... | collective-permute-start | bytes 1572872 | tf_op jit(solution)/shard_map/ppermute | solution.py:267
  9.5 2.6 %collective-permute-start.1 = (f32[1,2,256,256]{3,2,1,0:T(8,128)S(1)}, f32[1,2,256,256]{3,2,1,0:T(8,128)S(1)}, u32[]{:S(2)}, u32[]{:S(2)}) collective-permute-start(f32[1,2,256,256]{3,2,1,0:T(8,128)S(1)} %get-tuple-element.32), channel_id=1, source_target_pairs={{0,128},{64,192},{128,0},{192,64},{1,129},{65,193},{129,1},{193,65... | collective-permute-start | bytes 1572872 | tf_op jit(solution)/shard_map/ppermute | solution.py:267
  12.2 2.0 %collective-permute-start.7 = (f32[3,64,256]{2,1,0:T(8,128)S(1)}, f32[3,64,256]{2,1,0:T(8,128)S(1)}, u32[]{:S(2)}, u32[]{:S(2)}) collective-permute-start(f32[3,64,256]{2,1,0:T(8,128)S(1)} %constant_dynamic-update-slice_fusion.refs_8_), channel_id=1, source_target_pairs={{0,2},{1,3},{2,0},{3,1},{4,6},{5,7},{6,4},{7,5},{8,10},{9,11},{10,... | collective-permute-start | bytes 589832 | tf_op jit(solution)/shard_map/ppermute | solution.py:292
  14.3 4.5 %collective-permute-done.8.refs_11_ = f32[3,64,256]{2,1,0:T(8,128)S(1)} collective-permute-done((f32[3,64,256]{2,1,0:T(8,128)S(1)}, f32[3,64,256]{2,1,0:T(8,128)S(1)}, u32[]{:S(2)}, u32[]{:S(2)}) %collective-permute-start.8) | collective-permute-done | bytes 196640 | tf_op jit(solution)/shard_map/ppermute | solution.py:292
  18.7 1.6 %copy-done.1 = f32[4,2,256,256]{3,2,1,0:T(8,128)S(1)} copy-done((f32[4,2,256,256]{3,2,1,0:T(8,128)S(1)}, f32[4,2,256,256]{3,2,1,0:T(8,128)}, u32[]{:S(2)}) %copy-start.1) | copy-done | bytes 2097176
  20.5 2.0 %collective-permute-done.2.refs_7_ = f32[1,2,256,256]{3,2,1,0:T(8,128)S(1)} collective-permute-done((f32[1,2,256,256]{3,2,1,0:T(8,128)S(1)}, f32[1,2,256,256]{3,2,1,0:T(8,128)S(1)}, u32[]{:S(2)}, u32[]{:S(2)}) %collective-permute-start.2) | collective-permute-done | bytes 524320 | tf_op jit(solution)/shard_map/ppermute | solution.py:267
  22.4 1.3 %collective-permute-done.refs_5_ = f32[1,2,256,256]{3,2,1,0:T(8,128)S(1)} collective-permute-done((f32[1,2,256,256]{3,2,1,0:T(8,128)S(1)}, f32[1,2,256,256]{3,2,1,0:T(8,128)S(1)}, u32[]{:S(2)}, u32[]{:S(2)}) %collective-permute-start) | collective-permute-done | bytes 524320 | tf_op jit(solution)/shard_map/ppermute | solution.py:267
  23.7 9.5 %collective-permute-done.1.refs_6_ = f32[1,2,256,256]{3,2,1,0:T(8,128)S(1)} collective-permute-done((f32[1,2,256,256]{3,2,1,0:T(8,128)S(1)}, f32[1,2,256,256]{3,2,1,0:T(8,128)S(1)}, u32[]{:S(2)}, u32[]{:S(2)}) %collective-permute-start.1) | collective-permute-done | bytes 524320 | tf_op jit(solution)/shard_map/ppermute | solution.py:267
  33.3 5.2 %chain.1 = (f32[1,2,256,256]{3,2,1,0:T(8,128)S(1)}, f32[1,2,256,256]{3,2,1,0:T(8,128)S(1)}, f32[1,1,256,256]{3,2,1,0:T(8,128)S(1)}, f32[1,2,256,256]{3,2,1,0:T(8,128)S(1)}, f32[1,1,256,256]{3,2,1,0:T(8,128)S(1)}) custom-call(s32[1]{0:T(128)} %bitcast.me.refs_0_, s32[1]{0:T(128)} %bitcast.2.refs_1_, f32[2,256,256]{2,1,0:T(8,128)S(1)} %get-tuple-element.16.refs_2_, ...), custom_call_target="tpu_custom_call" | custom-call | flops 3221225472 | bytes 5242880 | tf_op jit(solution)/shard_map/chain/pallas_call | solution.py:120
  38.5 1.6 %collective-permute-start.9 = (f32[1,2,256,256]{3,2,1,0:T(8,128)S(1)}, f32[1,2,256,256]{3,2,1,0:T(8,128)S(1)}, u32[]{:S(2)}, u32[]{:S(2)}) collective-permute-start(f32[1,2,256,256]{3,2,1,0:T(8,128)S(1)} %get-tuple-element.20), channel_id=1, source_target_pairs={{0,64},{64,128},{128,192},{192,0},{1,65},{65,129},{129,193},{193,1... | collective-permute-start | bytes 1572872 | tf_op jit(solution)/shard_map/ppermute | solution.py:267
  40.9 5.7 %collective-permute-start.11 = (f32[1,2,256,256]{3,2,1,0:T(8,128)S(1)}, f32[1,2,256,256]{3,2,1,0:T(8,128)S(1)}, u32[]{:S(2)}, u32[]{:S(2)}) collective-permute-start(f32[1,2,256,256]{3,2,1,0:T(8,128)S(1)} %get-tuple-element.19.refs_2_), channel_id=1, source_target_pairs={{1,0},{2,1},{3,2},{4,3},{5,4},{6,5},{7,6},{8,7},{9,8},{10,9},{11,1... | collective-permute-start | bytes 1572872 | tf_op jit(solution)/shard_map/ppermute | solution.py:276
  46.7 4.8 %collective-permute-done.9.value = f32[1,2,256,256]{3,2,1,0:T(8,128)S(1)} collective-permute-done((f32[1,2,256,256]{3,2,1,0:T(8,128)S(1)}, f32[1,2,256,256]{3,2,1,0:T(8,128)S(1)}, u32[]{:S(2)}, u32[]{:S(2)}) %collective-permute-start.9) | collective-permute-done | bytes 524320 | tf_op jit(solution)/shard_map/ppermute | solution.py:267
  53.3 2.4 %collective-permute-start.14 = (f32[1,1,256,256]{3,2,1,0:T(8,128)S(1)}, f32[1,1,256,256]{3,2,1,0:T(8,128)S(1)}, u32[]{:S(2)}, u32[]{:S(2)}) collective-permute-start(f32[1,1,256,256]{3,2,1,0:T(8,128)S(1)} %get-tuple-element.25), channel_id=1, source_target_pairs={{0,128},{64,192},{128,0},{192,64},{1,129},{65,193},{129,1},{193,65... | collective-permute-start | bytes 786440 | tf_op jit(solution)/shard_map/ppermute | solution.py:267
  56.9 5.4 %collective-permute-start.12 = (f32[1,2,256,256]{3,2,1,0:T(8,128)S(1)}, f32[1,2,256,256]{3,2,1,0:T(8,128)S(1)}, u32[]{:S(2)}, u32[]{:S(2)}) collective-permute-start(f32[1,2,256,256]{3,2,1,0:T(8,128)S(1)} %admit.2.refs_3_), channel_id=1, source_target_pairs={{0,1},{1,2},{2,3},{3,4},{4,5},{5,6},{6,7},{7,8},{8,9},{9,10},{10,1... | collective-permute-start | bytes 1572872 | tf_op jit(solution)/shard_map/ppermute | solution.py:276
  62.2 1.9 %collective-permute-start.13 = (f32[1,2,256,256]{3,2,1,0:T(8,128)S(1)}, f32[1,2,256,256]{3,2,1,0:T(8,128)S(1)}, u32[]{:S(2)}, u32[]{:S(2)}) collective-permute-start(f32[1,2,256,256]{3,2,1,0:T(8,128)S(1)} %admit.3.refs_4_), channel_id=1, source_target_pairs={{1,0},{2,1},{3,2},{4,3},{5,4},{6,5},{7,6},{8,7},{9,8},{10,9},{11,1... | collective-permute-start | bytes 1572872 | tf_op jit(solution)/shard_map/ppermute | solution.py:276
  64.2 1.9 %collective-permute-start.16 = (f32[1,1,256,256]{3,2,1,0:T(8,128)S(1)}, f32[1,1,256,256]{3,2,1,0:T(8,128)S(1)}, u32[]{:S(2)}, u32[]{:S(2)}) collective-permute-start(f32[1,1,256,256]{3,2,1,0:T(8,128)S(1)} %collective-permute-done.14.refs_3_), channel_id=1, source_target_pairs={{0,1},{1,2},{2,3},{3,4},{4,5},{5,6},{6,7},{7,8},{8,9},{9,10},{10,1... | collective-permute-start | bytes 786440 | tf_op jit(solution)/shard_map/ppermute | solution.py:276
  67.3 1.9 %collective-permute-start.17 = (f32[1,1,256,256]{3,2,1,0:T(8,128)S(1)}, f32[1,1,256,256]{3,2,1,0:T(8,128)S(1)}, u32[]{:S(2)}, u32[]{:S(2)}) collective-permute-start(f32[1,1,256,256]{3,2,1,0:T(8,128)S(1)} %collective-permute-done.15.refs_4_), channel_id=1, source_target_pairs={{0,1},{1,2},{2,3},{3,4},{4,5},{5,6},{6,7},{7,8},{8,9},{9,10},{10,1... | collective-permute-start | bytes 786440 | tf_op jit(solution)/shard_map/ppermute | solution.py:276
  69.4 5.4 %collective-permute-done.13.refs_7_ = f32[1,2,256,256]{3,2,1,0:T(8,128)S(1)} collective-permute-done((f32[1,2,256,256]{3,2,1,0:T(8,128)S(1)}, f32[1,2,256,256]{3,2,1,0:T(8,128)S(1)}, u32[]{:S(2)}, u32[]{:S(2)}) %collective-permute-start.13) | collective-permute-done | bytes 524320 | tf_op jit(solution)/shard_map/ppermute | solution.py:276
  74.8 1.7 %band_early.1 = (f32[4,2,256,256]{3,2,1,0:T(8,128)}, f32[2,4,256,256]{3,2,1,0:T(8,128)S(1)}) custom-call(s32[1]{0:T(128)} %bitcast.me.refs_0_, f32[4,8]{1,0:T(4,128)S(1)} %select_reduce_fusion.refs_1_, f32[1,2,256,256]{3,2,1,0:T(8,128)S(1)} %get-tuple-element.19.refs_2_, f32[1,2,256,256]{3,2,1,0:T(8,128)S(1)} %admit.2.refs_3_, ...), custom_call_target="tpu_custom_call" | custom-call | bytes 4194304 | tf_op jit(solution)/shard_map/band_early/pallas_call | solution.py:178
  77.6 2.8 %collective-permute-done.17.refs_6_ = f32[1,1,256,256]{3,2,1,0:T(8,128)S(1)} collective-permute-done((f32[1,1,256,256]{3,2,1,0:T(8,128)S(1)}, f32[1,1,256,256]{3,2,1,0:T(8,128)S(1)}, u32[]{:S(2)}, u32[]{:S(2)}) %collective-permute-start.17) | collective-permute-done | bytes 262176 | tf_op jit(solution)/shard_map/ppermute | solution.py:276
  80.5 2.1 %band_late.1 = (f32[4,2,256,256]{3,2,1,0:T(8,128)}, f32[4,2,256,256]{3,2,1,0:T(8,128)}) custom-call(s32[1]{0:T(128)} %bitcast.me.refs_0_, f32[4,8]{1,0:T(4,128)S(1)} %select_reduce_fusion.refs_1_, f32[2,4,256,256]{3,2,1,0:T(8,128)S(1)} %get-tuple-element.22.refs_2_, ...), custom_call_target="tpu_custom_call", output_to_operand_aliasing={{0}: (7, {})} | custom-call | tf_op jit(solution)/shard_map/band_late/pallas_call | solution.py:225
  (37 shorter events, 8.5 us)
Async XLA Ops:
  0.6 18.1 %copy-start = (f32[1,4,2,256,256]{4,3,2,1,0:T(8,128)S(1)}, f32[1,4,2,256,256]{4,3,2,1,0:T(8,128)}, u32[]{:S(2)}) copy-start(f32[1,4,2,256,256]{4,3,2,1,0:T(8,128)} %param.5) | copy-start | bytes 6291460
  3.2 6.3 %collective-permute-start.3 = (f32[1,64,256]{2,1,0:T(8,128)S(1)}, f32[1,64,256]{2,1,0:T(8,128)S(1)}, u32[]{:S(2)}, u32[]{:S(2)}) collective-permute-start(f32[1,64,256]{2,1,0:T(8,128)S(1)} %constant_dynamic-slice_fusion), channel_id=1, source_target_pairs={{0,64},{64,128},{128,192},{192,0},{1,65},{65,129},{129,193},{193,1... | collective-permute-start | bytes 196616 | tf_op jit(solution)/shard_map/ppermute | solution.py:267
  4.8 7.3 %collective-permute-start.5 = (f32[1,64,256]{2,1,0:T(8,128)S(1)}, f32[1,64,256]{2,1,0:T(8,128)S(1)}, u32[]{:S(2)}, u32[]{:S(2)}) collective-permute-start(f32[1,64,256]{2,1,0:T(8,128)S(1)} %constant_dynamic-slice_fusion), channel_id=1, source_target_pairs={{0,192},{64,0},{128,64},{192,128},{1,193},{65,1},{129,65},{193,129... | collective-permute-start | bytes 196616 | tf_op jit(solution)/shard_map/ppermute | solution.py:267
  5.3 6.8 %collective-permute-start.4 = (f32[1,64,256]{2,1,0:T(8,128)S(1)}, f32[1,64,256]{2,1,0:T(8,128)S(1)}, u32[]{:S(2)}, u32[]{:S(2)}) collective-permute-start(f32[1,64,256]{2,1,0:T(8,128)S(1)} %constant_dynamic-slice_fusion), channel_id=1, source_target_pairs={{0,128},{64,192},{128,0},{192,64},{1,129},{65,193},{129,1},{193,65... | collective-permute-start | bytes 196616 | tf_op jit(solution)/shard_map/ppermute | solution.py:267
  7.4 15.0 %collective-permute-start.2 = (f32[1,2,256,256]{3,2,1,0:T(8,128)S(1)}, f32[1,2,256,256]{3,2,1,0:T(8,128)S(1)}, u32[]{:S(2)}, u32[]{:S(2)}) collective-permute-start(f32[1,2,256,256]{3,2,1,0:T(8,128)S(1)} %get-tuple-element.30), channel_id=1, source_target_pairs={{0,192},{64,0},{128,64},{192,128},{1,193},{65,1},{129,65},{193,129... | collective-permute-start | bytes 1572872 | tf_op jit(solution)/shard_map/ppermute | solution.py:267
  8.9 14.9 %collective-permute-start = (f32[1,2,256,256]{3,2,1,0:T(8,128)S(1)}, f32[1,2,256,256]{3,2,1,0:T(8,128)S(1)}, u32[]{:S(2)}, u32[]{:S(2)}) collective-permute-start(f32[1,2,256,256]{3,2,1,0:T(8,128)S(1)} %get-tuple-element.31), channel_id=1, source_target_pairs={{0,64},{64,128},{128,192},{192,0},{1,65},{65,129},{129,193},{193,1... | collective-permute-start | bytes 1572872 | tf_op jit(solution)/shard_map/ppermute | solution.py:267
  9.5 23.8 %collective-permute-start.1 = (f32[1,2,256,256]{3,2,1,0:T(8,128)S(1)}, f32[1,2,256,256]{3,2,1,0:T(8,128)S(1)}, u32[]{:S(2)}, u32[]{:S(2)}) collective-permute-start(f32[1,2,256,256]{3,2,1,0:T(8,128)S(1)} %get-tuple-element.32), channel_id=1, source_target_pairs={{0,128},{64,192},{128,0},{192,64},{1,129},{65,193},{129,1},{193,65... | collective-permute-start | bytes 1572872 | tf_op jit(solution)/shard_map/ppermute | solution.py:267
  12.1 6.6 %collective-permute-start.8 = (f32[3,64,256]{2,1,0:T(8,128)S(1)}, f32[3,64,256]{2,1,0:T(8,128)S(1)}, u32[]{:S(2)}, u32[]{:S(2)}) collective-permute-start(f32[3,64,256]{2,1,0:T(8,128)S(1)} %constant_dynamic-update-slice_fusion.refs_8_), channel_id=1, source_target_pairs={{0,17},{1,16},{2,19},{3,18},{4,21},{5,20},{6,23},{7,22},{8,25},{9,... | collective-permute-start | bytes 589832 | tf_op jit(solution)/shard_map/ppermute | solution.py:292
  12.2 8.2 %collective-permute-start.7 = (f32[3,64,256]{2,1,0:T(8,128)S(1)}, f32[3,64,256]{2,1,0:T(8,128)S(1)}, u32[]{:S(2)}, u32[]{:S(2)}) collective-permute-start(f32[3,64,256]{2,1,0:T(8,128)S(1)} %constant_dynamic-update-slice_fusion.refs_8_), channel_id=1, source_target_pairs={{0,2},{1,3},{2,0},{3,1},{4,6},{5,7},{6,4},{7,5},{8,10},{9,11},{10,... | collective-permute-start | bytes 589832 | tf_op jit(solution)/shard_map/ppermute | solution.py:292
  18.7 1.7 %collective-permute-start.6 = (f32[3,64,256]{2,1,0:T(8,128)S(1)}, f32[3,64,256]{2,1,0:T(8,128)S(1)}, u32[]{:S(2)}, u32[]{:S(2)}) collective-permute-start(f32[3,64,256]{2,1,0:T(8,128)S(1)} %constant_dynamic-update-slice_fusion.refs_8_), channel_id=1, source_target_pairs={{0,1},{1,0},{2,3},{3,2},{4,5},{5,4},{6,7},{7,6},{8,9},{9,8},{10,11... | collective-permute-start | bytes 589832 | tf_op jit(solution)/shard_map/ppermute | solution.py:292
  18.7 1.6 %copy-start.1 = (f32[4,2,256,256]{3,2,1,0:T(8,128)S(1)}, f32[4,2,256,256]{3,2,1,0:T(8,128)}, u32[]{:S(2)}) copy-start(f32[4,2,256,256]{3,2,1,0:T(8,128)} %boundary_all.1) | copy-start | bytes 6291460
  20.3 12.9 %copy-start.2 = (f32[1,256,256]{2,1,0:T(8,128)S(1)}, f32[1,256,256]{2,1,0:T(8,128)}, u32[]{:S(2)}) copy-start(f32[1,256,256]{2,1,0:T(8,128)} %refs_4_.1) | copy-start | bytes 786436
  38.5 13.0 %collective-permute-start.9 = (f32[1,2,256,256]{3,2,1,0:T(8,128)S(1)}, f32[1,2,256,256]{3,2,1,0:T(8,128)S(1)}, u32[]{:S(2)}, u32[]{:S(2)}) collective-permute-start(f32[1,2,256,256]{3,2,1,0:T(8,128)S(1)} %get-tuple-element.20), channel_id=1, source_target_pairs={{0,64},{64,128},{128,192},{192,0},{1,65},{65,129},{129,193},{193,1... | collective-permute-start | bytes 1572872 | tf_op jit(solution)/shard_map/ppermute | solution.py:267
  40.1 12.1 %collective-permute-start.10 = (f32[1,2,256,256]{3,2,1,0:T(8,128)S(1)}, f32[1,2,256,256]{3,2,1,0:T(8,128)S(1)}, u32[]{:S(2)}, u32[]{:S(2)}) collective-permute-start(f32[1,2,256,256]{3,2,1,0:T(8,128)S(1)} %get-tuple-element.21), channel_id=1, source_target_pairs={{0,192},{64,0},{128,64},{192,128},{1,193},{65,1},{129,65},{193,129... | collective-permute-start | bytes 1572872 | tf_op jit(solution)/shard_map/ppermute | solution.py:267
  40.9 12.4 %collective-permute-start.11 = (f32[1,2,256,256]{3,2,1,0:T(8,128)S(1)}, f32[1,2,256,256]{3,2,1,0:T(8,128)S(1)}, u32[]{:S(2)}, u32[]{:S(2)}) collective-permute-start(f32[1,2,256,256]{3,2,1,0:T(8,128)S(1)} %get-tuple-element.19.refs_2_), channel_id=1, source_target_pairs={{1,0},{2,1},{3,2},{4,3},{5,4},{6,5},{7,6},{8,7},{9,8},{10,9},{11,1... | collective-permute-start | bytes 1572872 | tf_op jit(solution)/shard_map/ppermute | solution.py:276
  51.5 17.8 %copy-start.3 = (f32[1,6]{1,0:T(1,128)S(1)}, f32[1,6]{1,0:T(1,128)}, u32[]{:S(2)}) copy-start(f32[1,6]{1,0:T(1,128)} %param.9) | copy-start | bytes 76
  51.5 17.8 %copy-start.4 = (s32[6]{0:T(128)S(1)}, s32[6]{0:T(128)}, u32[]{:S(2)}) copy-start(s32[6]{0:T(128)} %param.8) | copy-start | bytes 76
  53.3 10.9 %collective-permute-start.14 = (f32[1,1,256,256]{3,2,1,0:T(8,128)S(1)}, f32[1,1,256,256]{3,2,1,0:T(8,128)S(1)}, u32[]{:S(2)}, u32[]{:S(2)}) collective-permute-start(f32[1,1,256,256]{3,2,1,0:T(8,128)S(1)} %get-tuple-element.25), channel_id=1, source_target_pairs={{0,128},{64,192},{128,0},{192,64},{1,129},{65,193},{129,1},{193,65... | collective-permute-start | bytes 786440 | tf_op jit(solution)/shard_map/ppermute | solution.py:267
  55.8 11.6 %collective-permute-start.15 = (f32[1,1,256,256]{3,2,1,0:T(8,128)S(1)}, f32[1,1,256,256]{3,2,1,0:T(8,128)S(1)}, u32[]{:S(2)}, u32[]{:S(2)}) collective-permute-start(f32[1,1,256,256]{3,2,1,0:T(8,128)S(1)} %get-tuple-element.26), channel_id=1, source_target_pairs={{0,128},{64,192},{128,0},{192,64},{1,129},{65,193},{129,1},{193,65... | collective-permute-start | bytes 786440 | tf_op jit(solution)/shard_map/ppermute | solution.py:267
  56.9 12.5 %collective-permute-start.12 = (f32[1,2,256,256]{3,2,1,0:T(8,128)S(1)}, f32[1,2,256,256]{3,2,1,0:T(8,128)S(1)}, u32[]{:S(2)}, u32[]{:S(2)}) collective-permute-start(f32[1,2,256,256]{3,2,1,0:T(8,128)S(1)} %admit.2.refs_3_), channel_id=1, source_target_pairs={{0,1},{1,2},{2,3},{3,4},{4,5},{5,6},{6,7},{7,8},{8,9},{9,10},{10,1... | collective-permute-start | bytes 1572872 | tf_op jit(solution)/shard_map/ppermute | solution.py:276
  62.2 12.6 %collective-permute-start.13 = (f32[1,2,256,256]{3,2,1,0:T(8,128)S(1)}, f32[1,2,256,256]{3,2,1,0:T(8,128)S(1)}, u32[]{:S(2)}, u32[]{:S(2)}) collective-permute-start(f32[1,2,256,256]{3,2,1,0:T(8,128)S(1)} %admit.3.refs_4_), channel_id=1, source_target_pairs={{1,0},{2,1},{3,2},{4,3},{5,4},{6,5},{7,6},{8,7},{9,8},{10,9},{11,1... | collective-permute-start | bytes 1572872 | tf_op jit(solution)/shard_map/ppermute | solution.py:276
  64.2 13.4 %collective-permute-start.16 = (f32[1,1,256,256]{3,2,1,0:T(8,128)S(1)}, f32[1,1,256,256]{3,2,1,0:T(8,128)S(1)}, u32[]{:S(2)}, u32[]{:S(2)}) collective-permute-start(f32[1,1,256,256]{3,2,1,0:T(8,128)S(1)} %collective-permute-done.14.refs_3_), channel_id=1, source_target_pairs={{0,1},{1,2},{2,3},{3,4},{4,5},{5,6},{6,7},{7,8},{8,9},{9,10},{10,1... | collective-permute-start | bytes 786440 | tf_op jit(solution)/shard_map/ppermute | solution.py:276
  67.3 13.1 %collective-permute-start.17 = (f32[1,1,256,256]{3,2,1,0:T(8,128)S(1)}, f32[1,1,256,256]{3,2,1,0:T(8,128)S(1)}, u32[]{:S(2)}, u32[]{:S(2)}) collective-permute-start(f32[1,1,256,256]{3,2,1,0:T(8,128)S(1)} %collective-permute-done.15.refs_4_), channel_id=1, source_target_pairs={{0,1},{1,2},{2,3},{3,4},{4,5},{5,6},{6,7},{7,8},{8,9},{9,10},{10,1... | collective-permute-start | bytes 786440 | tf_op jit(solution)/shard_map/ppermute | solution.py:276

commit v2 on v1

--- a/solution.py
+++ b/solution.py
@@ -16,6 +16,7 @@
 EARLY = (0, 1, 3)
 ROWS = 32
 LATE = 2
+FIRST = 3
 SMALL = pltpu.CompilerParams(vmem_limit_bytes=8 * 1024 * 1024)
 def split(value):
     high = value.astype(BF16)
@@ -70,25 +71,48 @@
     )(me, inverse_blocks, boundary)
 
 
-def chain_kernel(parts, me_ref, quarter_ref, kept, start, own_coupling, *refs):
-    arrived = refs[: parts - 1]
-    quarters = refs[parts - 1 : 2 * parts - 1]
-    outs = refs[2 * parts - 1 : 3 * parts]
-    high, low, inverse, previous, coupling = refs[3 * parts :]
+def prepare_kernel(parts, me_ref, quarter_ref, kept, own_coupling, arrived, *refs):
+    quarters = refs[:parts]
+    high, low, inverse, coupling = refs[parts:]
     me = me_ref[0]
-    orb = coupling.shape[-1]
-    rows = orb // len(quarters)
-
+    rows = coupling.shape[-1] // len(quarters)
     coupling[0] = own_coupling[0]
     for number, source in enumerate(quarters):
         quarter = lax.bitwise_xor(quarter_ref[0], number)
         place = pl.ds(pl.multiple_of(quarter * rows, rows), rows)
         for shift in range(1, parts):
             coupling[shift, place, :] = source[shift - 1]
-    for shift in range(parts):
+    for shift, block in ((0, kept[...]), (FIRST, arrived[0])):
         stage = lax.rem(me - shift + parts, parts)
-        inverse[stage] = kept[...] if shift == 0 else arrived[shift - 1][0]
-        store_transfer(inverse[stage], coupling[shift], high, low, stage)
+        inverse[stage] = block
+        store_transfer(block, coupling[shift], high, low, stage)
+
+
+def run_prepare(me, quarter, kept, coupling, arrived, quarters):
+    parts, orb = len(quarters), kept.shape[-1]
+    return pl.pallas_call(
+        lambda *refs: prepare_kernel(parts, *refs),
+        out_shape=[
+            jax.ShapeDtypeStruct((parts, 3, orb, orb), BF16),
+            jax.ShapeDtypeStruct((parts, 3, orb, orb), BF16),
+            jax.ShapeDtypeStruct((parts, 2, orb, orb), F32),
+            jax.ShapeDtypeStruct((parts, orb, orb), F32),
+        ],
+        in_specs=[SMEM] * 2 + [VMEM] * (3 + parts),
+        out_specs=[VMEM] * 4,
+        compiler_params=PARAMS,
+        name="prepare",
+    )(me, quarter, kept, coupling, arrived, *quarters)
+
+
+def chain_kernel(parts, me_ref, start, coupling, first, second, *refs):
+    high, low, inverse = refs[3:6]
+    outs, previous = refs[6:-1], refs[-1]
+    me = me_ref[0]
+    for shift, block in zip([shift for shift in range(1, parts) if shift != FIRST], (first, second)):
+        stage = lax.rem(me - shift + parts, parts)
+        inverse[stage] = block[0]
+        store_transfer(block[0], coupling[shift], high, low, stage)
     previous[...] = start[...]
     for stage in range(parts):
         transfer = [(high[stage, number], low[stage, number]) for number in range(3)]
@@ -111,24 +135,20 @@
                     outs[number][0, 1] = imag
 
 
-def run_chain(me, quarter, kept, start, coupling, arrived, quarters):
-    parts = len(arrived) + 1
-    orb = start.shape[-1]
-    outs = [jax.ShapeDtypeStruct((1, 2, orb, orb), F32)] * parts
-    outs[LATE] = jax.ShapeDtypeStruct((1, 1, orb, orb), F32)
-    outs.append(outs[LATE])
+def run_chain(me, start, prepared, arrived):
+    high, low, inverse, coupling = prepared
+    parts, orb = high.shape[0], high.shape[-1]
+    outs = [jax.ShapeDtypeStruct(value.shape, value.dtype) for value in (high, low, inverse)]
+    outs += [jax.ShapeDtypeStruct((1, 2, orb, orb), F32)] * parts
+    outs[3 + LATE] = jax.ShapeDtypeStruct((1, 1, orb, orb), F32)
+    outs.append(outs[3 + LATE])
     return pl.pallas_call(
         lambda *refs: chain_kernel(parts, *refs),
         out_shape=outs,
-        in_specs=[SMEM] * 2 + [VMEM] * (3 + len(arrived) + len(quarters)),
-        out_specs=[VMEM] * (parts + 1),
-        scratch_shapes=[
-            pltpu.VMEM((parts, 3, orb, orb), BF16),
-            pltpu.VMEM((parts, 3, orb, orb), BF16),
-            pltpu.VMEM((parts, 2, orb, orb), F32),
-            pltpu.VMEM((2, orb, orb), F32),
-            pltpu.VMEM((parts, orb, orb), F32),
-        ],
+        in_specs=[SMEM] + [VMEM] * 7,
+        out_specs=[VMEM] * len(outs),
+        input_output_aliases={5: 0, 6: 1, 7: 2},
+        scratch_shapes=[pltpu.VMEM((2, orb, orb), F32)],
         compiler_params=PARAMS,
         cost_estimate=pl.CostEstimate(
             flops=parts * 48 * orb**3,
@@ -136,7 +156,7 @@
             transcendentals=0,
         ),
         name="chain",
-    )(me, quarter, kept, start, coupling, *arrived, *quarters)
+    )(me, start, coupling, *arrived, high, low, inverse)[3:]
 
 
 def mix(weights, columns, values, row):
@@ -294,7 +314,10 @@
     ]
     kept, start = run_pick(me[None], own_inverse, boundary)
 
-    produced = run_chain(me[None], quarter[None], kept, start, coupling, arrived, quarters)
+    prepared = run_prepare(
+        me[None], quarter[None], kept, coupling, arrived.pop(FIRST - 1), quarters
+    )
+    produced = run_chain(me[None], start, prepared, arrived)
     early = [produced[0]] + [ring(produced[shift], shift) for shift in EARLY[1:]]
     halos = [halo(early[0], 0)]
     early[1:] = [run_admit(value) for value in early[1:]]

time: 82.9 us -> 82.1 us (level)
  transfers between devices with their start and end apart: 18 -> 18, of which waited for: 11 -> 12; matrix products, arithmetic and copies ran while one was open for 0% -> 0% of each run, Pallas kernels for 2% -> 3%
where the time goes in v2:
time: 82.1 us; the launch traced here: 81.8 us
  waiting for transfers between devices  34.1 us (42%)
  starting transfers between devices  33.3 us (41%)
  Pallas kernels  9.21 us (11%)
  local copies, waits for them, and re-layouts  4.15 us (5%)
  between operations  0.86 us (1%)
    ppermute x10, waiting for transfers between devices, ring(): return lax.ppermute(value, 'sec', pairs)  19.1 us
    ppermute x5, starting transfers between devices, halo(): return lax.ppermute(value, both, pairs)  16.7 us
    ppermute x10, starting transfers between devices, ring(): return lax.ppermute(value, 'sec', pairs)  14 us
    ppermute x5, waiting for transfers between devices, halo(): return lax.ppermute(value, both, pairs)  10.4 us
    ppermute x3, waiting for transfers between devices, on_device(): lax.ppermute(first, 'en', [(source, source ^ partner) for source in range...  4.68 us
    pallas_call x1, Pallas kernels, run_chain(): pl.pallas_call(lambda *refs: chain_kernel(parts, *refs), out_shape=outs,...  4.46 us
    ppermute x3, starting transfers between devices, on_device(): lax.ppermute(first, 'en', [(source, source ^ partner) for source in range...  2.59 us
    pallas_call x1, Pallas kernels, run_late(): pl.pallas_call(lambda *refs: late_kernel(count, *refs), out_shape=[whole]...  2.12 us
  transfers between devices with their start and end apart: 18, of which 12 were waited for; matrix products, arithmetic and copies ran while one was open for 0% of the time, Pallas kernels for 3%

profile of v2, /device:TPU:26, one launch (start us, length us, event | category | flops | bytes accessed | tf_op | source)
XLA Modules:
  0.0 81.8 jit_solution(2574601897041648478)
XLA Ops:
  1.7 1.5 %dynamic-slice_bitcast_fusion = (f32[1,2,256,256]{3,2,1,0:T(8,128)S(1)}, f32[1,2,256,256]{3,2,1,0:T(8,128)S(1)}, f32[1,2,256,256]{3,2,1,0:T(8,128)S(1)}) fusion(f32[1,4,2,256,256]{4,3,2,1,0:T(8,128)} %param.5, s32[]{:T(128)S(6)} %select_n.30, s32[]{:T(128)S(6)} %select_n.27, s32[]{:T(128)S(6)} %select_n.29), kind=kLoop, calls=%fused_computation | loop fusion | bytes 3145740 | tf_op jit(solution)/shard_map/dynamic_slice | solution.py:302
  3.2 1.6 %collective-permute-start.1 = (f32[1,64,256]{2,1,0:T(8,128)S(1)}, f32[1,64,256]{2,1,0:T(8,128)S(1)}, u32[]{:S(2)}, u32[]{:S(2)}) collective-permute-start(f32[1,64,256]{2,1,0:T(8,128)S(1)} %constant_dynamic-slice_fusion), channel_id=1, source_target_pairs={{0,64},{64,128},{128,192},{192,0},{1,65},{65,129},{129,193},{193,1... | collective-permute-start | bytes 196616 | tf_op jit(solution)/shard_map/ppermute | solution.py:287
  5.9 2.2 %collective-permute-start.3 = (f32[1,64,256]{2,1,0:T(8,128)S(1)}, f32[1,64,256]{2,1,0:T(8,128)S(1)}, u32[]{:S(2)}, u32[]{:S(2)}) collective-permute-start(f32[1,64,256]{2,1,0:T(8,128)S(1)} %constant_dynamic-slice_fusion), channel_id=1, source_target_pairs={{0,192},{64,0},{128,64},{192,128},{1,193},{65,1},{129,65},{193,129... | collective-permute-start | bytes 196616 | tf_op jit(solution)/shard_map/ppermute | solution.py:287
  8.1 1.4 %collective-permute-start = (f32[1,2,256,256]{3,2,1,0:T(8,128)S(1)}, f32[1,2,256,256]{3,2,1,0:T(8,128)S(1)}, u32[]{:S(2)}, u32[]{:S(2)}) collective-permute-start(f32[1,2,256,256]{3,2,1,0:T(8,128)S(1)} %get-tuple-element.39), channel_id=1, source_target_pairs={{0,192},{64,0},{128,64},{192,128},{1,193},{65,1},{129,65},{193,129... | collective-permute-start | bytes 1572872 | tf_op jit(solution)/shard_map/ppermute | solution.py:287
  10.1 1.5 %collective-permute-start.8 = (f32[1,2,256,256]{3,2,1,0:T(8,128)S(1)}, f32[1,2,256,256]{3,2,1,0:T(8,128)S(1)}, u32[]{:S(2)}, u32[]{:S(2)}) collective-permute-start(f32[1,2,256,256]{3,2,1,0:T(8,128)S(1)} %get-tuple-element.38), channel_id=1, source_target_pairs={{0,128},{64,192},{128,0},{192,64},{1,129},{65,193},{129,1},{193,65... | collective-permute-start | bytes 1572872 | tf_op jit(solution)/shard_map/ppermute | solution.py:287
  11.7 2.0 %collective-permute-start.5 = (f32[3,64,256]{2,1,0:T(8,128)S(1)}, f32[3,64,256]{2,1,0:T(8,128)S(1)}, u32[]{:S(2)}, u32[]{:S(2)}) collective-permute-start(f32[3,64,256]{2,1,0:T(8,128)S(1)} %constant_dynamic-update-slice_fusion.refs_5_), channel_id=1, source_target_pairs={{0,2},{1,3},{2,0},{3,1},{4,6},{5,7},{6,4},{7,5},{8,10},{9,11},{10,... | collective-permute-start | bytes 589832 | tf_op jit(solution)/shard_map/ppermute | solution.py:312
  14.3 1.6 %copy-done.1 = f32[4,2,256,256]{3,2,1,0:T(8,128)S(1)} copy-done((f32[4,2,256,256]{3,2,1,0:T(8,128)S(1)}, f32[4,2,256,256]{3,2,1,0:T(8,128)}, u32[]{:S(2)}) %copy-start.1) | copy-done | bytes 2097176
  15.9 3.3 %collective-permute-done.5.refs_7_ = f32[3,64,256]{2,1,0:T(8,128)S(1)} collective-permute-done((f32[3,64,256]{2,1,0:T(8,128)S(1)}, f32[3,64,256]{2,1,0:T(8,128)S(1)}, u32[]{:S(2)}, u32[]{:S(2)}) %collective-permute-start.5) | collective-permute-done | bytes 196640 | tf_op jit(solution)/shard_map/ppermute | solution.py:312
  19.2 1.4 %collective-permute-done.6.refs_8_ = f32[3,64,256]{2,1,0:T(8,128)S(1)} collective-permute-done((f32[3,64,256]{2,1,0:T(8,128)S(1)}, f32[3,64,256]{2,1,0:T(8,128)S(1)}, u32[]{:S(2)}, u32[]{:S(2)}) %collective-permute-start.6) | collective-permute-done | bytes 196640 | tf_op jit(solution)/shard_map/ppermute | solution.py:312
  20.6 2.6 %collective-permute-done.refs_4_ = f32[1,2,256,256]{3,2,1,0:T(8,128)S(1)} collective-permute-done((f32[1,2,256,256]{3,2,1,0:T(8,128)S(1)}, f32[1,2,256,256]{3,2,1,0:T(8,128)S(1)}, u32[]{:S(2)}, u32[]{:S(2)}) %collective-permute-start) | collective-permute-done | bytes 524320 | tf_op jit(solution)/shard_map/ppermute | solution.py:287
  24.3 9.4 %collective-permute-done.8.refs_4_ = f32[1,2,256,256]{3,2,1,0:T(8,128)S(1)} collective-permute-done((f32[1,2,256,256]{3,2,1,0:T(8,128)S(1)}, f32[1,2,256,256]{3,2,1,0:T(8,128)S(1)}, u32[]{:S(2)}, u32[]{:S(2)}) %collective-permute-start.8) | collective-permute-done | bytes 524320 | tf_op jit(solution)/shard_map/ppermute | solution.py:287
  33.7 4.5 %chain.1 = (bf16[4,3,256,256]{3,2,1,0:T(8,128)(2,1)S(1)}, bf16[4,3,256,256]{3,2,1,0:T(8,128)(2,1)S(1)}, f32[4,2,256,256]{3,2,1,0:T(8,128)S(1)}, f32[1,2,256,256]...) custom-call(s32[1]{0:T(128)} %bitcast.me.refs_0_, ...), custom_call_target="tpu_custom_call", output_to_operand_aliasing={{0}: (5, {}), {1}: (6, {}), {2}: (7, {})} | custom-call | flops 3221225472 | bytes 5242880 | tf_op jit(solution)/shard_map/chain/pallas_call | solution.py:145
  40.3 5.6 %collective-permute-start.11 = (f32[1,2,256,256]{3,2,1,0:T(8,128)S(1)}, f32[1,2,256,256]{3,2,1,0:T(8,128)S(1)}, u32[]{:S(2)}, u32[]{:S(2)}) collective-permute-start(f32[1,2,256,256]{3,2,1,0:T(8,128)S(1)} %get-tuple-element.27.refs_2_), channel_id=1, source_target_pairs={{1,0},{2,1},{3,2},{4,3},{5,4},{6,5},{7,6},{8,7},{9,8},{10,9},{11,1... | collective-permute-start | bytes 1572872 | tf_op jit(solution)/shard_map/ppermute | solution.py:296
  45.9 4.8 %collective-permute-done.9.value = f32[1,2,256,256]{3,2,1,0:T(8,128)S(1)} collective-permute-done((f32[1,2,256,256]{3,2,1,0:T(8,128)S(1)}, f32[1,2,256,256]{3,2,1,0:T(8,128)S(1)}, u32[]{:S(2)}, u32[]{:S(2)}) %collective-permute-start.9) | collective-permute-done | bytes 524320 | tf_op jit(solution)/shard_map/ppermute | solution.py:287
  52.6 2.4 %collective-permute-start.14 = (f32[1,1,256,256]{3,2,1,0:T(8,128)S(1)}, f32[1,1,256,256]{3,2,1,0:T(8,128)S(1)}, u32[]{:S(2)}, u32[]{:S(2)}) collective-permute-start(f32[1,1,256,256]{3,2,1,0:T(8,128)S(1)} %get-tuple-element.33), channel_id=1, source_target_pairs={{0,128},{64,192},{128,0},{192,64},{1,129},{65,193},{129,1},{193,65... | collective-permute-start | bytes 786440 | tf_op jit(solution)/shard_map/ppermute | solution.py:287
  56.1 5.4 %collective-permute-start.12 = (f32[1,2,256,256]{3,2,1,0:T(8,128)S(1)}, f32[1,2,256,256]{3,2,1,0:T(8,128)S(1)}, u32[]{:S(2)}, u32[]{:S(2)}) collective-permute-start(f32[1,2,256,256]{3,2,1,0:T(8,128)S(1)} %admit.2.refs_3_), channel_id=1, source_target_pairs={{0,1},{1,2},{2,3},{3,4},{4,5},{5,6},{6,7},{7,8},{8,9},{9,10},{10,1... | collective-permute-start | bytes 1572872 | tf_op jit(solution)/shard_map/ppermute | solution.py:296
  61.5 1.9 %collective-permute-start.13 = (f32[1,2,256,256]{3,2,1,0:T(8,128)S(1)}, f32[1,2,256,256]{3,2,1,0:T(8,128)S(1)}, u32[]{:S(2)}, u32[]{:S(2)}) collective-permute-start(f32[1,2,256,256]{3,2,1,0:T(8,128)S(1)} %admit.3.refs_4_), channel_id=1, source_target_pairs={{1,0},{2,1},{3,2},{4,3},{5,4},{6,5},{7,6},{8,7},{9,8},{10,9},{11,1... | collective-permute-start | bytes 1572872 | tf_op jit(solution)/shard_map/ppermute | solution.py:296
  63.5 1.9 %collective-permute-start.16 = (f32[1,1,256,256]{3,2,1,0:T(8,128)S(1)}, f32[1,1,256,256]{3,2,1,0:T(8,128)S(1)}, u32[]{:S(2)}, u32[]{:S(2)}) collective-permute-start(f32[1,1,256,256]{3,2,1,0:T(8,128)S(1)} %collective-permute-done.14.refs_3_), channel_id=1, source_target_pairs={{0,1},{1,2},{2,3},{3,4},{4,5},{5,6},{6,7},{7,8},{8,9},{9,10},{10,1... | collective-permute-start | bytes 786440 | tf_op jit(solution)/shard_map/ppermute | solution.py:296
  65.4 1.3 %collective-permute-done.15.refs_4_ = f32[1,1,256,256]{3,2,1,0:T(8,128)S(1)} collective-permute-done((f32[1,1,256,256]{3,2,1,0:T(8,128)S(1)}, f32[1,1,256,256]{3,2,1,0:T(8,128)S(1)}, u32[]{:S(2)}, u32[]{:S(2)}) %collective-permute-start.15) | collective-permute-done | bytes 262176 | tf_op jit(solution)/shard_map/ppermute | solution.py:287
  66.7 1.9 %collective-permute-start.17 = (f32[1,1,256,256]{3,2,1,0:T(8,128)S(1)}, f32[1,1,256,256]{3,2,1,0:T(8,128)S(1)}, u32[]{:S(2)}, u32[]{:S(2)}) collective-permute-start(f32[1,1,256,256]{3,2,1,0:T(8,128)S(1)} %collective-permute-done.15.refs_4_), channel_id=1, source_target_pairs={{0,1},{1,2},{2,3},{3,4},{4,5},{5,6},{6,7},{7,8},{8,9},{9,10},{10,1... | collective-permute-start | bytes 786440 | tf_op jit(solution)/shard_map/ppermute | solution.py:296
  68.7 5.3 %collective-permute-done.13.refs_7_ = f32[1,2,256,256]{3,2,1,0:T(8,128)S(1)} collective-permute-done((f32[1,2,256,256]{3,2,1,0:T(8,128)S(1)}, f32[1,2,256,256]{3,2,1,0:T(8,128)S(1)}, u32[]{:S(2)}, u32[]{:S(2)}) %collective-permute-start.13) | collective-permute-done | bytes 524320 | tf_op jit(solution)/shard_map/ppermute | solution.py:296
  74.1 1.7 %band_early.1 = (f32[4,2,256,256]{3,2,1,0:T(8,128)}, f32[2,4,256,256]{3,2,1,0:T(8,128)S(1)}) custom-call(s32[1]{0:T(128)} %bitcast.me.refs_0_, f32[4,8]{1,0:T(4,128)S(1)} %select_reduce_fusion.refs_1_, f32[1,2,256,256]{3,2,1,0:T(8,128)S(1)} %get-tuple-element.27.refs_2_, f32[1,2,256,256]{3,2,1,0:T(8,128)S(1)} %admit.2.refs_3_, ...), custom_call_target="tpu_custom_call" | custom-call | bytes 4194304 | tf_op jit(solution)/shard_map/band_early/pallas_call | solution.py:198
  76.9 2.8 %collective-permute-done.17.refs_6_ = f32[1,1,256,256]{3,2,1,0:T(8,128)S(1)} collective-permute-done((f32[1,1,256,256]{3,2,1,0:T(8,128)S(1)}, f32[1,1,256,256]{3,2,1,0:T(8,128)S(1)}, u32[]{:S(2)}, u32[]{:S(2)}) %collective-permute-start.17) | collective-permute-done | bytes 262176 | tf_op jit(solution)/shard_map/ppermute | solution.py:296
  79.7 2.1 %band_late.1 = (f32[4,2,256,256]{3,2,1,0:T(8,128)}, f32[4,2,256,256]{3,2,1,0:T(8,128)}) custom-call(s32[1]{0:T(128)} %bitcast.me.refs_0_, f32[4,8]{1,0:T(4,128)S(1)} %select_reduce_fusion.refs_1_, f32[2,4,256,256]{3,2,1,0:T(8,128)S(1)} %get-tuple-element.30.refs_2_, ...), custom_call_target="tpu_custom_call", output_to_operand_aliasing={{0}: (7, {})} | custom-call | tf_op jit(solution)/shard_map/band_late/pallas_call | solution.py:245
  (38 shorter events, 11.0 us)
Async XLA Ops:
  0.6 13.6 %copy-start = (f32[1,4,2,256,256]{4,3,2,1,0:T(8,128)S(1)}, f32[1,4,2,256,256]{4,3,2,1,0:T(8,128)}, u32[]{:S(2)}) copy-start(f32[1,4,2,256,256]{4,3,2,1,0:T(8,128)} %param.5) | copy-start | bytes 6291460
  3.2 6.9 %collective-permute-start.1 = (f32[1,64,256]{2,1,0:T(8,128)S(1)}, f32[1,64,256]{2,1,0:T(8,128)S(1)}, u32[]{:S(2)}, u32[]{:S(2)}) collective-permute-start(f32[1,64,256]{2,1,0:T(8,128)S(1)} %constant_dynamic-slice_fusion), channel_id=1, source_target_pairs={{0,64},{64,128},{128,192},{192,0},{1,65},{65,129},{129,193},{193,1... | collective-permute-start | bytes 196616 | tf_op jit(solution)/shard_map/ppermute | solution.py:287
  4.8 6.8 %collective-permute-start.2 = (f32[1,64,256]{2,1,0:T(8,128)S(1)}, f32[1,64,256]{2,1,0:T(8,128)S(1)}, u32[]{:S(2)}, u32[]{:S(2)}) collective-permute-start(f32[1,64,256]{2,1,0:T(8,128)S(1)} %constant_dynamic-slice_fusion), channel_id=1, source_target_pairs={{0,128},{64,192},{128,0},{192,64},{1,129},{65,193},{129,1},{193,65... | collective-permute-start | bytes 196616 | tf_op jit(solution)/shard_map/ppermute | solution.py:287
  5.9 5.7 %collective-permute-start.3 = (f32[1,64,256]{2,1,0:T(8,128)S(1)}, f32[1,64,256]{2,1,0:T(8,128)S(1)}, u32[]{:S(2)}, u32[]{:S(2)}) collective-permute-start(f32[1,64,256]{2,1,0:T(8,128)S(1)} %constant_dynamic-slice_fusion), channel_id=1, source_target_pairs={{0,192},{64,0},{128,64},{192,128},{1,193},{65,1},{129,65},{193,129... | collective-permute-start | bytes 196616 | tf_op jit(solution)/shard_map/ppermute | solution.py:287
  8.1 15.1 %collective-permute-start = (f32[1,2,256,256]{3,2,1,0:T(8,128)S(1)}, f32[1,2,256,256]{3,2,1,0:T(8,128)S(1)}, u32[]{:S(2)}, u32[]{:S(2)}) collective-permute-start(f32[1,2,256,256]{3,2,1,0:T(8,128)S(1)} %get-tuple-element.39), channel_id=1, source_target_pairs={{0,192},{64,0},{128,64},{192,128},{1,193},{65,1},{129,65},{193,129... | collective-permute-start | bytes 1572872 | tf_op jit(solution)/shard_map/ppermute | solution.py:287
  9.5 14.9 %collective-permute-start.7 = (f32[1,2,256,256]{3,2,1,0:T(8,128)S(1)}, f32[1,2,256,256]{3,2,1,0:T(8,128)S(1)}, u32[]{:S(2)}, u32[]{:S(2)}) collective-permute-start(f32[1,2,256,256]{3,2,1,0:T(8,128)S(1)} %get-tuple-element.40), channel_id=1, source_target_pairs={{0,64},{64,128},{128,192},{192,0},{1,65},{65,129},{129,193},{193,1... | collective-permute-start | bytes 1572872 | tf_op jit(solution)/shard_map/ppermute | solution.py:287
  10.1 23.6 %collective-permute-start.8 = (f32[1,2,256,256]{3,2,1,0:T(8,128)S(1)}, f32[1,2,256,256]{3,2,1,0:T(8,128)S(1)}, u32[]{:S(2)}, u32[]{:S(2)}) collective-permute-start(f32[1,2,256,256]{3,2,1,0:T(8,128)S(1)} %get-tuple-element.38), channel_id=1, source_target_pairs={{0,128},{64,192},{128,0},{192,64},{1,129},{65,193},{129,1},{193,65... | collective-permute-start | bytes 1572872 | tf_op jit(solution)/shard_map/ppermute | solution.py:287
  11.6 2.1 %collective-permute-start.4 = (f32[3,64,256]{2,1,0:T(8,128)S(1)}, f32[3,64,256]{2,1,0:T(8,128)S(1)}, u32[]{:S(2)}, u32[]{:S(2)}) collective-permute-start(f32[3,64,256]{2,1,0:T(8,128)S(1)} %constant_dynamic-update-slice_fusion.refs_5_), channel_id=1, source_target_pairs={{0,1},{1,0},{2,3},{3,2},{4,5},{5,4},{6,7},{7,6},{8,9},{9,8},{10,11... | collective-permute-start | bytes 589832 | tf_op jit(solution)/shard_map/ppermute | solution.py:312
  11.7 7.5 %collective-permute-start.5 = (f32[3,64,256]{2,1,0:T(8,128)S(1)}, f32[3,64,256]{2,1,0:T(8,128)S(1)}, u32[]{:S(2)}, u32[]{:S(2)}) collective-permute-start(f32[3,64,256]{2,1,0:T(8,128)S(1)} %constant_dynamic-update-slice_fusion.refs_5_), channel_id=1, source_target_pairs={{0,2},{1,3},{2,0},{3,1},{4,6},{5,7},{6,4},{7,5},{8,10},{9,11},{10,... | collective-permute-start | bytes 589832 | tf_op jit(solution)/shard_map/ppermute | solution.py:312
  13.7 6.9 %collective-permute-start.6 = (f32[3,64,256]{2,1,0:T(8,128)S(1)}, f32[3,64,256]{2,1,0:T(8,128)S(1)}, u32[]{:S(2)}, u32[]{:S(2)}) collective-permute-start(f32[3,64,256]{2,1,0:T(8,128)S(1)} %constant_dynamic-update-slice_fusion.refs_5_), channel_id=1, source_target_pairs={{0,17},{1,16},{2,19},{3,18},{4,21},{5,20},{6,23},{7,22},{8,25},{9,... | collective-permute-start | bytes 589832 | tf_op jit(solution)/shard_map/ppermute | solution.py:312
  14.2 1.6 %copy-start.1 = (f32[4,2,256,256]{3,2,1,0:T(8,128)S(1)}, f32[4,2,256,256]{3,2,1,0:T(8,128)}, u32[]{:S(2)}) copy-start(f32[4,2,256,256]{3,2,1,0:T(8,128)} %boundary_all.1) | copy-start | bytes 6291460
  15.8 7.3 %copy-start.2 = (f32[1,256,256]{2,1,0:T(8,128)S(1)}, f32[1,256,256]{2,1,0:T(8,128)}, u32[]{:S(2)}) copy-start(f32[1,256,256]{2,1,0:T(8,128)} %refs_3_.1) | copy-start | bytes 786436
  38.2 12.5 %collective-permute-start.9 = (f32[1,2,256,256]{3,2,1,0:T(8,128)S(1)}, f32[1,2,256,256]{3,2,1,0:T(8,128)S(1)}, u32[]{:S(2)}, u32[]{:S(2)}) collective-permute-start(f32[1,2,256,256]{3,2,1,0:T(8,128)S(1)} %get-tuple-element.28), channel_id=1, source_target_pairs={{0,64},{64,128},{128,192},{192,0},{1,65},{65,129},{129,193},{193,1... | collective-permute-start | bytes 1572872 | tf_op jit(solution)/shard_map/ppermute | solution.py:287
  39.3 12.2 %collective-permute-start.10 = (f32[1,2,256,256]{3,2,1,0:T(8,128)S(1)}, f32[1,2,256,256]{3,2,1,0:T(8,128)S(1)}, u32[]{:S(2)}, u32[]{:S(2)}) collective-permute-start(f32[1,2,256,256]{3,2,1,0:T(8,128)S(1)} %get-tuple-element.29), channel_id=1, source_target_pairs={{0,192},{64,0},{128,64},{192,128},{1,193},{65,1},{129,65},{193,129... | collective-permute-start | bytes 1572872 | tf_op jit(solution)/shard_map/ppermute | solution.py:287
  40.3 12.3 %collective-permute-start.11 = (f32[1,2,256,256]{3,2,1,0:T(8,128)S(1)}, f32[1,2,256,256]{3,2,1,0:T(8,128)S(1)}, u32[]{:S(2)}, u32[]{:S(2)}) collective-permute-start(f32[1,2,256,256]{3,2,1,0:T(8,128)S(1)} %get-tuple-element.27.refs_2_), channel_id=1, source_target_pairs={{1,0},{2,1},{3,2},{4,3},{5,4},{6,5},{7,6},{8,7},{9,8},{10,9},{11,1... | collective-permute-start | bytes 1572872 | tf_op jit(solution)/shard_map/ppermute | solution.py:296
  50.7 17.9 %copy-start.3 = (f32[1,6]{1,0:T(1,128)S(1)}, f32[1,6]{1,0:T(1,128)}, u32[]{:S(2)}) copy-start(f32[1,6]{1,0:T(1,128)} %param.9) | copy-start | bytes 76
  50.7 17.9 %copy-start.4 = (s32[6]{0:T(128)S(1)}, s32[6]{0:T(128)}, u32[]{:S(2)}) copy-start(s32[6]{0:T(128)} %param.8) | copy-start | bytes 76
  52.6 10.9 %collective-permute-start.14 = (f32[1,1,256,256]{3,2,1,0:T(8,128)S(1)}, f32[1,1,256,256]{3,2,1,0:T(8,128)S(1)}, u32[]{:S(2)}, u32[]{:S(2)}) collective-permute-start(f32[1,1,256,256]{3,2,1,0:T(8,128)S(1)} %get-tuple-element.33), channel_id=1, source_target_pairs={{0,128},{64,192},{128,0},{192,64},{1,129},{65,193},{129,1},{193,65... | collective-permute-start | bytes 786440 | tf_op jit(solution)/shard_map/ppermute | solution.py:287
  55.0 11.7 %collective-permute-start.15 = (f32[1,1,256,256]{3,2,1,0:T(8,128)S(1)}, f32[1,1,256,256]{3,2,1,0:T(8,128)S(1)}, u32[]{:S(2)}, u32[]{:S(2)}) collective-permute-start(f32[1,1,256,256]{3,2,1,0:T(8,128)S(1)} %get-tuple-element.34), channel_id=1, source_target_pairs={{0,128},{64,192},{128,0},{192,64},{1,129},{65,193},{129,1},{193,65... | collective-permute-start | bytes 786440 | tf_op jit(solution)/shard_map/ppermute | solution.py:287
  56.1 12.6 %collective-permute-start.12 = (f32[1,2,256,256]{3,2,1,0:T(8,128)S(1)}, f32[1,2,256,256]{3,2,1,0:T(8,128)S(1)}, u32[]{:S(2)}, u32[]{:S(2)}) collective-permute-start(f32[1,2,256,256]{3,2,1,0:T(8,128)S(1)} %admit.2.refs_3_), channel_id=1, source_target_pairs={{0,1},{1,2},{2,3},{3,4},{4,5},{5,6},{6,7},{7,8},{8,9},{9,10},{10,1... | collective-permute-start | bytes 1572872 | tf_op jit(solution)/shard_map/ppermute | solution.py:296
  61.5 12.6 %collective-permute-start.13 = (f32[1,2,256,256]{3,2,1,0:T(8,128)S(1)}, f32[1,2,256,256]{3,2,1,0:T(8,128)S(1)}, u32[]{:S(2)}, u32[]{:S(2)}) collective-permute-start(f32[1,2,256,256]{3,2,1,0:T(8,128)S(1)} %admit.3.refs_4_), channel_id=1, source_target_pairs={{1,0},{2,1},{3,2},{4,3},{5,4},{6,5},{7,6},{8,7},{9,8},{10,9},{11,1... | collective-permute-start | bytes 1572872 | tf_op jit(solution)/shard_map/ppermute | solution.py:296
  63.5 13.4 %collective-permute-start.16 = (f32[1,1,256,256]{3,2,1,0:T(8,128)S(1)}, f32[1,1,256,256]{3,2,1,0:T(8,128)S(1)}, u32[]{:S(2)}, u32[]{:S(2)}) collective-permute-start(f32[1,1,256,256]{3,2,1,0:T(8,128)S(1)} %collective-permute-done.14.refs_3_), channel_id=1, source_target_pairs={{0,1},{1,2},{2,3},{3,4},{4,5},{5,6},{6,7},{7,8},{8,9},{9,10},{10,1... | collective-permute-start | bytes 786440 | tf_op jit(solution)/shard_map/ppermute | solution.py:296
  66.7 13.0 %collective-permute-start.17 = (f32[1,1,256,256]{3,2,1,0:T(8,128)S(1)}, f32[1,1,256,256]{3,2,1,0:T(8,128)S(1)}, u32[]{:S(2)}, u32[]{:S(2)}) collective-permute-start(f32[1,1,256,256]{3,2,1,0:T(8,128)S(1)} %collective-permute-done.15.refs_4_), channel_id=1, source_target_pairs={{0,1},{1,2},{2,3},{3,4},{4,5},{5,6},{6,7},{7,8},{8,9},{9,10},{10,1... | collective-permute-start | bytes 786440 | tf_op jit(solution)/shard_map/ppermute | solution.py:296

commit v3 on v2

--- a/solution.py
+++ b/solution.py
@@ -166,92 +166,114 @@
     return total
 
 
-def early_kernel(count, scalars, weights, *refs):
-    slots = refs[: 2 * len(EARLY)]
-    green, partial, sems = refs[2 * len(EARLY) :]
-    me = scalars[0]
-    orb = partial.shape[-1]
+def touched(me, count):
+    return jnp.where(lax.rem(me - LATE + count, count) >= count // 2, 0, count // 2)
+
+
+def early_kernel(count, me_ref, weights, *refs):
+    wide = len(EARLY)
+    slots, halos, late = refs[:wide], refs[wide : 2 * wide], refs[2 * wide : 2 * wide + 2]
+    green, energy, rest, done, sems = refs[2 * wide + 2 :]
+    me = me_ref[0]
+    pair = count // 2
+    orb = rest.shape[-1]
     copies = []
     for number, shift in enumerate(EARLY):
         place = lax.rem(me - shift + count, count)
-        copies.append(pltpu.make_async_copy(slots[number].at[0], green.at[place], sems.at[number]))
+        copies.append(
+            pltpu.make_async_copy(slots[number].at[0], green.at[place], sems.at[pair + number])
+        )
+    place = lax.rem(me - LATE + count, count)
+    for half in range(2):
+        copies.append(
+            pltpu.make_async_copy(
+                late[half].at[0, 0], green.at[place, half], sems.at[pair + wide + half]
+            )
+        )
     for copy in copies:
         copy.start()
-    columns = list(EARLY) + [count + shift for shift in EARLY]
-    rows = 32
-    for half in range(2):
-
-        @pl.loop(0, orb // rows)
-        def _(step):
-            place = pl.ds(pl.multiple_of(step * rows, rows), rows)
-            values = [slot[0, half, place, :] for slot in slots]
-            for row in range(count):
-                partial[half, row, place, :] = mix(weights, columns, values, row)
-
-    for copy in copies:
-        copy.wait()
-
-
-def run_early(me, weights, slots):
-    count = weights.shape[0]
-    orb = slots[0].shape[-1]
-    return pl.pallas_call(
-        lambda *refs: early_kernel(count, *refs),
-        out_shape=[
-            jax.ShapeDtypeStruct((count, 2, orb, orb), F32),
-            jax.ShapeDtypeStruct((2, count, orb, orb), F32),
-        ],
-        in_specs=[SMEM, SMEM] + [VMEM] * len(slots),
-        out_specs=[HBM, VMEM],
-        scratch_shapes=[pltpu.SemaphoreType.DMA((len(EARLY),))],
-        compiler_params=SMALL,
-        cost_estimate=pl.CostEstimate(
-            flops=0, bytes_accessed=64 * orb * orb, transcendentals=0
-        ),
-        name="band_early",
-    )(me[None], weights, *slots)
-
-
-def late_kernel(count, me_ref, weights, partial, *refs):
-    slots, halos = refs[:2], refs[2:4]
-    green, energy, done, sems = refs[5:]
-    orb = partial.shape[-1]
-    place = lax.rem(me_ref[0] - LATE + count, count)
-    copies = []
-    for half, slot in enumerate(slots):
-        copies.append(pltpu.make_async_copy(slot.at[0, 0], green.at[place, half], sems.at[half]))
-        copies[-1].start()
-    for row in range(count):
+    base = touched(me, count)
+    columns = list(EARLY) + [count + shift for shift in EARLY] + [LATE]
+    for target, first in ((done, pair - base), (rest, base)):
         for half in range(2):
 
             @pl.loop(0, orb // ROWS)
             def _(step):
                 where = pl.ds(pl.multiple_of(step * ROWS, ROWS), ROWS)
-                values = [slots[half][0, 0, where, :], halos[half][0, 0, where, :]]
-                done[row, half, where, :] = partial[half, row, where, :] + mix(
-                    weights, (LATE, count + LATE), values, row
+                values = [ref[0, half, where, :] for ref in slots + halos]
+                values.append(late[half][0, 0, where, :])
+                for number in range(pair):
+                    target[number, half, where, :] = mix(weights, columns, values, first + number)
+
+        if target is done:
+            for number in range(pair):
+                copy = pltpu.make_async_copy(
+                    done.at[number], energy.at[first + number], sems.at[number]
                 )
-
-        copy = pltpu.make_async_copy(done.at[row], energy.at[row], sems.at[2 + row])
+                copy.start()
+                copies.append(copy)
+    for copy in copies:
+        copy.wait()
+
+
+def run_early(me, weights, slots, late):
+    count = weights.shape[0]
+    orb = slots[0].shape[-1]
+    whole = jax.ShapeDtypeStruct((count, 2, orb, orb), F32)
+    pair = (count // 2, 2, orb, orb)
+    return pl.pallas_call(
+        lambda *refs: early_kernel(count, *refs),
+        out_shape=[whole, whole, jax.ShapeDtypeStruct(pair, F32)],
+        in_specs=[SMEM, SMEM] + [VMEM] * (len(slots) + 2),
+        out_specs=[HBM, HBM, VMEM],
+        scratch_shapes=[
+            pltpu.VMEM(pair, F32),
+            pltpu.SemaphoreType.DMA((count // 2 + len(EARLY) + 2,)),
+        ],
+        compiler_params=SMALL,
+        cost_estimate=pl.CostEstimate(flops=0, bytes_accessed=64 * orb * orb, transcendentals=0),
+        name="band_early",
+    )(me[None], weights, *slots, *late)
+
+
+def late_kernel(count, me_ref, weights, rest, real, imag, _, energy, done, sems):
+    orb = rest.shape[-1]
+    base = touched(me_ref[0], count)
+    copies = []
+    for number in range(count // 2):
+        row = base + number
+        for half, halo in enumerate((real, imag)):
+
+            @pl.loop(0, orb // ROWS)
+            def _(step):
+                where = pl.ds(pl.multiple_of(step * ROWS, ROWS), ROWS)
+                done[number, half, where, :] = (
+                    rest[number, half, where, :]
+                    + weights[row, count + LATE] * halo[0, 0, where, :]
+                )
+
+        copy = pltpu.make_async_copy(done.at[number], energy.at[row], sems.at[number])
         copy.start()
         copies.append(copy)
     for copy in copies:
         copy.wait()
 
 
-def run_late(me, weights, partial, slots, halos, green):
+def run_late(me, weights, rest, halos, energy):
     count = weights.shape[0]
-    whole = jax.ShapeDtypeStruct(green.shape, F32)
     return pl.pallas_call(
         lambda *refs: late_kernel(count, *refs),
-        out_shape=[whole] * 2,
-        in_specs=[SMEM, SMEM] + [VMEM] * 5 + [HBM],
-        out_specs=[HBM] * 2,
-        input_output_aliases={7: 0},
-        scratch_shapes=[pltpu.VMEM(green.shape, F32), pltpu.SemaphoreType.DMA((2 + count,))],
+        out_shape=jax.ShapeDtypeStruct(energy.shape, F32),
+        in_specs=[SMEM, SMEM] + [VMEM] * 3 + [HBM],
+        out_specs=HBM,
+        input_output_aliases={5: 0},
+        scratch_shapes=[
+            pltpu.VMEM(rest.shape, F32),
+            pltpu.SemaphoreType.DMA((count // 2,)),
+        ],
         compiler_params=SMALL,
         name="band_late",
-    )(me[None], weights, partial, *slots, *halos, green)
+    )(me[None], weights, rest, *halos, energy)
 
 
 def admit_kernel(value, kept):
@@ -332,8 +354,8 @@
     away = place[None, :] - jnp.arange(count, dtype=jnp.int32)[:, None]
     hits = (band_offsets[:, None, None] == away[None]).astype(F32)
     weights = jnp.sum(band_weights[0][:, None, None] * hits, axis=0)
-    green, partial = run_early(me, weights, early + halos)
-    green, energy = run_late(me, weights, partial, late, late_halos, green)
+    green, energy, rest = run_early(me, weights, early + halos, late)
+    energy = run_late(me, weights, rest, late_halos, energy)
     return green[None], energy[None]
 
 

time: 82.1 us -> 81.7 us (level)
  transfers between devices with their start and end apart: 18 -> 18, of which waited for: 12 -> 12; matrix products, arithmetic and copies ran while one was open for 0% -> 0% of each run, Pallas kernels for 3% -> 4%
where the time goes in v3:
time: 81.7 us; the launch traced here: 81.4 us
  waiting for transfers between devices  33.6 us (41%)
  starting transfers between devices  33.3 us (41%)
  Pallas kernels  9.33 us (11%)
  local copies, waits for them, and re-layouts  4.15 us (5%)
  between operations  0.86 us (1%)
    ppermute x10, waiting for transfers between devices, ring(): return lax.ppermute(value, 'sec', pairs)  19.1 us
    ppermute x5, starting transfers between devices, halo(): return lax.ppermute(value, both, pairs)  16.7 us
    ppermute x10, starting transfers between devices, ring(): return lax.ppermute(value, 'sec', pairs)  14 us
    ppermute x5, waiting for transfers between devices, halo(): return lax.ppermute(value, both, pairs)  9.81 us
    ppermute x3, waiting for transfers between devices, on_device(): lax.ppermute(first, 'en', [(source, source ^ partner) for source in range...  4.68 us
    pallas_call x1, Pallas kernels, run_chain(): pl.pallas_call(lambda *refs: chain_kernel(parts, *refs), out_shape=outs,...  4.46 us
    ppermute x3, starting transfers between devices, on_device(): lax.ppermute(first, 'en', [(source, source ^ partner) for source in range...  2.59 us
    pallas_call x1, Pallas kernels, run_early(): pl.pallas_call(lambda *refs: early_kernel(count, *refs), out_shape=[whole...  2.28 us
  transfers between devices with their start and end apart: 18, of which 12 were waited for; matrix products, arithmetic and copies ran while one was open for 0% of the time, Pallas kernels for 4%

profile of v3, /device:TPU:26, one launch (start us, length us, event | category | flops | bytes accessed | tf_op | source)
XLA Modules:
  0.0 81.4 jit_solution(16050434449317548112)
XLA Ops:
  1.7 1.5 %dynamic-slice_bitcast_fusion = (f32[1,2,256,256]{3,2,1,0:T(8,128)S(1)}, f32[1,2,256,256]{3,2,1,0:T(8,128)S(1)}, f32[1,2,256,256]{3,2,1,0:T(8,128)S(1)}) fusion(f32[1,4,2,256,256]{4,3,2,1,0:T(8,128)} %param.5, s32[]{:T(128)S(6)} %select_n.30, s32[]{:T(128)S(6)} %select_n.27, s32[]{:T(128)S(6)} %select_n.29), kind=kLoop, calls=%fused_computation | loop fusion | bytes 3145740 | tf_op jit(solution)/shard_map/dynamic_slice | solution.py:324
  3.2 1.6 %collective-permute-start.1 = (f32[1,64,256]{2,1,0:T(8,128)S(1)}, f32[1,64,256]{2,1,0:T(8,128)S(1)}, u32[]{:S(2)}, u32[]{:S(2)}) collective-permute-start(f32[1,64,256]{2,1,0:T(8,128)S(1)} %constant_dynamic-slice_fusion), channel_id=1, source_target_pairs={{0,64},{64,128},{128,192},{192,0},{1,65},{65,129},{129,193},{193,1... | collective-permute-start | bytes 196616 | tf_op jit(solution)/shard_map/ppermute | solution.py:309
  5.9 2.2 %collective-permute-start.3 = (f32[1,64,256]{2,1,0:T(8,128)S(1)}, f32[1,64,256]{2,1,0:T(8,128)S(1)}, u32[]{:S(2)}, u32[]{:S(2)}) collective-permute-start(f32[1,64,256]{2,1,0:T(8,128)S(1)} %constant_dynamic-slice_fusion), channel_id=1, source_target_pairs={{0,192},{64,0},{128,64},{192,128},{1,193},{65,1},{129,65},{193,129... | collective-permute-start | bytes 196616 | tf_op jit(solution)/shard_map/ppermute | solution.py:309
  8.1 1.4 %collective-permute-start = (f32[1,2,256,256]{3,2,1,0:T(8,128)S(1)}, f32[1,2,256,256]{3,2,1,0:T(8,128)S(1)}, u32[]{:S(2)}, u32[]{:S(2)}) collective-permute-start(f32[1,2,256,256]{3,2,1,0:T(8,128)S(1)} %get-tuple-element.37), channel_id=1, source_target_pairs={{0,192},{64,0},{128,64},{192,128},{1,193},{65,1},{129,65},{193,129... | collective-permute-start | bytes 1572872 | tf_op jit(solution)/shard_map/ppermute | solution.py:309
  10.1 1.5 %collective-permute-start.8 = (f32[1,2,256,256]{3,2,1,0:T(8,128)S(1)}, f32[1,2,256,256]{3,2,1,0:T(8,128)S(1)}, u32[]{:S(2)}, u32[]{:S(2)}) collective-permute-start(f32[1,2,256,256]{3,2,1,0:T(8,128)S(1)} %get-tuple-element.36), channel_id=1, source_target_pairs={{0,128},{64,192},{128,0},{192,64},{1,129},{65,193},{129,1},{193,65... | collective-permute-start | bytes 1572872 | tf_op jit(solution)/shard_map/ppermute | solution.py:309
  11.7 2.0 %collective-permute-start.5 = (f32[3,64,256]{2,1,0:T(8,128)S(1)}, f32[3,64,256]{2,1,0:T(8,128)S(1)}, u32[]{:S(2)}, u32[]{:S(2)}) collective-permute-start(f32[3,64,256]{2,1,0:T(8,128)S(1)} %constant_dynamic-update-slice_fusion.refs_5_), channel_id=1, source_target_pairs={{0,2},{1,3},{2,0},{3,1},{4,6},{5,7},{6,4},{7,5},{8,10},{9,11},{10,... | collective-permute-start | bytes 589832 | tf_op jit(solution)/shard_map/ppermute | solution.py:334
  14.3 1.6 %copy-done.1 = f32[4,2,256,256]{3,2,1,0:T(8,128)S(1)} copy-done((f32[4,2,256,256]{3,2,1,0:T(8,128)S(1)}, f32[4,2,256,256]{3,2,1,0:T(8,128)}, u32[]{:S(2)}) %copy-start.1) | copy-done | bytes 2097176
  15.9 3.3 %collective-permute-done.5.refs_7_ = f32[3,64,256]{2,1,0:T(8,128)S(1)} collective-permute-done((f32[3,64,256]{2,1,0:T(8,128)S(1)}, f32[3,64,256]{2,1,0:T(8,128)S(1)}, u32[]{:S(2)}, u32[]{:S(2)}) %collective-permute-start.5) | collective-permute-done | bytes 196640 | tf_op jit(solution)/shard_map/ppermute | solution.py:334
  19.2 1.4 %collective-permute-done.6.refs_8_ = f32[3,64,256]{2,1,0:T(8,128)S(1)} collective-permute-done((f32[3,64,256]{2,1,0:T(8,128)S(1)}, f32[3,64,256]{2,1,0:T(8,128)S(1)}, u32[]{:S(2)}, u32[]{:S(2)}) %collective-permute-start.6) | collective-permute-done | bytes 196640 | tf_op jit(solution)/shard_map/ppermute | solution.py:334
  20.6 2.6 %collective-permute-done.refs_4_ = f32[1,2,256,256]{3,2,1,0:T(8,128)S(1)} collective-permute-done((f32[1,2,256,256]{3,2,1,0:T(8,128)S(1)}, f32[1,2,256,256]{3,2,1,0:T(8,128)S(1)}, u32[]{:S(2)}, u32[]{:S(2)}) %collective-permute-start) | collective-permute-done | bytes 524320 | tf_op jit(solution)/shard_map/ppermute | solution.py:309
  24.3 9.4 %collective-permute-done.8.refs_4_ = f32[1,2,256,256]{3,2,1,0:T(8,128)S(1)} collective-permute-done((f32[1,2,256,256]{3,2,1,0:T(8,128)S(1)}, f32[1,2,256,256]{3,2,1,0:T(8,128)S(1)}, u32[]{:S(2)}, u32[]{:S(2)}) %collective-permute-start.8) | collective-permute-done | bytes 524320 | tf_op jit(solution)/shard_map/ppermute | solution.py:309
  33.7 4.5 %chain.1 = (bf16[4,3,256,256]{3,2,1,0:T(8,128)(2,1)S(1)}, bf16[4,3,256,256]{3,2,1,0:T(8,128)(2,1)S(1)}, f32[4,2,256,256]{3,2,1,0:T(8,128)S(1)}, f32[1,2,256,256]...) custom-call(s32[1]{0:T(128)} %bitcast.me.refs_0_, ...), custom_call_target="tpu_custom_call", output_to_operand_aliasing={{0}: (5, {}), {1}: (6, {}), {2}: (7, {})} | custom-call | flops 3221225472 | bytes 5242880 | tf_op jit(solution)/shard_map/chain/pallas_call | solution.py:145
  40.3 5.6 %collective-permute-start.11 = (f32[1,2,256,256]{3,2,1,0:T(8,128)S(1)}, f32[1,2,256,256]{3,2,1,0:T(8,128)S(1)}, u32[]{:S(2)}, u32[]{:S(2)}) collective-permute-start(f32[1,2,256,256]{3,2,1,0:T(8,128)S(1)} %get-tuple-element.26.refs_2_), channel_id=1, source_target_pairs={{1,0},{2,1},{3,2},{4,3},{5,4},{6,5},{7,6},{8,7},{9,8},{10,9},{11,1... | collective-permute-start | bytes 1572872 | tf_op jit(solution)/shard_map/ppermute | solution.py:318
  45.9 4.8 %collective-permute-done.9.value = f32[1,2,256,256]{3,2,1,0:T(8,128)S(1)} collective-permute-done((f32[1,2,256,256]{3,2,1,0:T(8,128)S(1)}, f32[1,2,256,256]{3,2,1,0:T(8,128)S(1)}, u32[]{:S(2)}, u32[]{:S(2)}) %collective-permute-start.9) | collective-permute-done | bytes 524320 | tf_op jit(solution)/shard_map/ppermute | solution.py:309
  52.6 2.4 %collective-permute-start.14 = (f32[1,1,256,256]{3,2,1,0:T(8,128)S(1)}, f32[1,1,256,256]{3,2,1,0:T(8,128)S(1)}, u32[]{:S(2)}, u32[]{:S(2)}) collective-permute-start(f32[1,1,256,256]{3,2,1,0:T(8,128)S(1)} %get-tuple-element.31), channel_id=1, source_target_pairs={{0,128},{64,192},{128,0},{192,64},{1,129},{65,193},{129,1},{193,65... | collective-permute-start | bytes 786440 | tf_op jit(solution)/shard_map/ppermute | solution.py:309
  56.1 5.4 %collective-permute-start.12 = (f32[1,2,256,256]{3,2,1,0:T(8,128)S(1)}, f32[1,2,256,256]{3,2,1,0:T(8,128)S(1)}, u32[]{:S(2)}, u32[]{:S(2)}) collective-permute-start(f32[1,2,256,256]{3,2,1,0:T(8,128)S(1)} %admit.2.refs_3_), channel_id=1, source_target_pairs={{0,1},{1,2},{2,3},{3,4},{4,5},{5,6},{6,7},{7,8},{8,9},{9,10},{10,1... | collective-permute-start | bytes 1572872 | tf_op jit(solution)/shard_map/ppermute | solution.py:318
  61.5 1.9 %collective-permute-start.13 = (f32[1,2,256,256]{3,2,1,0:T(8,128)S(1)}, f32[1,2,256,256]{3,2,1,0:T(8,128)S(1)}, u32[]{:S(2)}, u32[]{:S(2)}) collective-permute-start(f32[1,2,256,256]{3,2,1,0:T(8,128)S(1)} %admit.3.refs_4_), channel_id=1, source_target_pairs={{1,0},{2,1},{3,2},{4,3},{5,4},{6,5},{7,6},{8,7},{9,8},{10,9},{11,1... | collective-permute-start | bytes 1572872 | tf_op jit(solution)/shard_map/ppermute | solution.py:318
  63.5 1.9 %collective-permute-start.16 = (f32[1,1,256,256]{3,2,1,0:T(8,128)S(1)}, f32[1,1,256,256]{3,2,1,0:T(8,128)S(1)}, u32[]{:S(2)}, u32[]{:S(2)}) collective-permute-start(f32[1,1,256,256]{3,2,1,0:T(8,128)S(1)} %collective-permute-done.14.refs_8_), channel_id=1, source_target_pairs={{0,1},{1,2},{2,3},{3,4},{4,5},{5,6},{6,7},{7,8},{8,9},{9,10},{10,1... | collective-permute-start | bytes 786440 | tf_op jit(solution)/shard_map/ppermute | solution.py:318
  65.4 1.3 %collective-permute-done.15.refs_9_ = f32[1,1,256,256]{3,2,1,0:T(8,128)S(1)} collective-permute-done((f32[1,1,256,256]{3,2,1,0:T(8,128)S(1)}, f32[1,1,256,256]{3,2,1,0:T(8,128)S(1)}, u32[]{:S(2)}, u32[]{:S(2)}) %collective-permute-start.15) | collective-permute-done | bytes 262176 | tf_op jit(solution)/shard_map/ppermute | solution.py:309
  66.7 1.9 %collective-permute-start.17 = (f32[1,1,256,256]{3,2,1,0:T(8,128)S(1)}, f32[1,1,256,256]{3,2,1,0:T(8,128)S(1)}, u32[]{:S(2)}, u32[]{:S(2)}) collective-permute-start(f32[1,1,256,256]{3,2,1,0:T(8,128)S(1)} %collective-permute-done.15.refs_9_), channel_id=1, source_target_pairs={{0,1},{1,2},{2,3},{3,4},{4,5},{5,6},{6,7},{7,8},{8,9},{9,10},{10,1... | collective-permute-start | bytes 786440 | tf_op jit(solution)/shard_map/ppermute | solution.py:318
  68.7 5.3 %collective-permute-done.13.refs_7_ = f32[1,2,256,256]{3,2,1,0:T(8,128)S(1)} collective-permute-done((f32[1,2,256,256]{3,2,1,0:T(8,128)S(1)}, f32[1,2,256,256]{3,2,1,0:T(8,128)S(1)}, u32[]{:S(2)}, u32[]{:S(2)}) %collective-permute-start.13) | collective-permute-done | bytes 524320 | tf_op jit(solution)/shard_map/ppermute | solution.py:318
  74.1 2.3 %band_early.1 = (f32[4,2,256,256]{3,2,1,0:T(8,128)}, f32[4,2,256,256]{3,2,1,0:T(8,128)}, f32[2,2,256,256]{3,2,1,0:T(8,128)S(1)}) custom-call(s32[1]{0:T(128)} %bitcast.me.refs_0_, f32[4,8]{1,0:T(4,128)S(1)} %select_reduce_fusion.refs_1_, f32[1,2,256,256]{3,2,1,0:T(8,128)S(1)} %get-tuple-element.26.refs_2_, f32[1,2,256,256]{3,2,1,0:T(8,128)S(1)} %admit.2.refs_3_, ...), custom_call_target="tpu_custom_call" | custom-call | bytes 4194304 | tf_op jit(solution)/shard_map/band_early/pallas_call | solution.py:224
  76.9 2.8 %collective-permute-done.17.refs_4_ = f32[1,1,256,256]{3,2,1,0:T(8,128)S(1)} collective-permute-done((f32[1,1,256,256]{3,2,1,0:T(8,128)S(1)}, f32[1,1,256,256]{3,2,1,0:T(8,128)S(1)}, u32[]{:S(2)}, u32[]{:S(2)}) %collective-permute-start.17) | collective-permute-done | bytes 262176 | tf_op jit(solution)/shard_map/ppermute | solution.py:318
  79.7 1.7 %band_late.1 = f32[4,2,256,256]{3,2,1,0:T(8,128)} custom-call(s32[1]{0:T(128)} %bitcast.me.refs_0_, f32[4,8]{1,0:T(4,128)S(1)} %select_reduce_fusion.refs_1_, f32[2,2,256,256]{3,2,1,0:T(8,128)S(1)} %get-tuple-element.34.refs_2_, f32[1,1,256,256]{3,2,1,0:T(8,128)S(1)} %collective-permute-done.16.refs_3_, ...), custom_call_target="tpu_custom_call", output_to_operand_aliasing={{}: (5, {})} | custom-call | tf_op jit(solution)/shard_map/band_late/pallas_call | solution.py:264
  (38 shorter events, 10.4 us)
Async XLA Ops:
  0.6 13.6 %copy-start = (f32[1,4,2,256,256]{4,3,2,1,0:T(8,128)S(1)}, f32[1,4,2,256,256]{4,3,2,1,0:T(8,128)}, u32[]{:S(2)}) copy-start(f32[1,4,2,256,256]{4,3,2,1,0:T(8,128)} %param.5) | copy-start | bytes 6291460
  3.2 6.9 %collective-permute-start.1 = (f32[1,64,256]{2,1,0:T(8,128)S(1)}, f32[1,64,256]{2,1,0:T(8,128)S(1)}, u32[]{:S(2)}, u32[]{:S(2)}) collective-permute-start(f32[1,64,256]{2,1,0:T(8,128)S(1)} %constant_dynamic-slice_fusion), channel_id=1, source_target_pairs={{0,64},{64,128},{128,192},{192,0},{1,65},{65,129},{129,193},{193,1... | collective-permute-start | bytes 196616 | tf_op jit(solution)/shard_map/ppermute | solution.py:309
  4.8 6.8 %collective-permute-start.2 = (f32[1,64,256]{2,1,0:T(8,128)S(1)}, f32[1,64,256]{2,1,0:T(8,128)S(1)}, u32[]{:S(2)}, u32[]{:S(2)}) collective-permute-start(f32[1,64,256]{2,1,0:T(8,128)S(1)} %constant_dynamic-slice_fusion), channel_id=1, source_target_pairs={{0,128},{64,192},{128,0},{192,64},{1,129},{65,193},{129,1},{193,65... | collective-permute-start | bytes 196616 | tf_op jit(solution)/shard_map/ppermute | solution.py:309
  5.9 5.7 %collective-permute-start.3 = (f32[1,64,256]{2,1,0:T(8,128)S(1)}, f32[1,64,256]{2,1,0:T(8,128)S(1)}, u32[]{:S(2)}, u32[]{:S(2)}) collective-permute-start(f32[1,64,256]{2,1,0:T(8,128)S(1)} %constant_dynamic-slice_fusion), channel_id=1, source_target_pairs={{0,192},{64,0},{128,64},{192,128},{1,193},{65,1},{129,65},{193,129... | collective-permute-start | bytes 196616 | tf_op jit(solution)/shard_map/ppermute | solution.py:309
  8.1 15.1 %collective-permute-start = (f32[1,2,256,256]{3,2,1,0:T(8,128)S(1)}, f32[1,2,256,256]{3,2,1,0:T(8,128)S(1)}, u32[]{:S(2)}, u32[]{:S(2)}) collective-permute-start(f32[1,2,256,256]{3,2,1,0:T(8,128)S(1)} %get-tuple-element.37), channel_id=1, source_target_pairs={{0,192},{64,0},{128,64},{192,128},{1,193},{65,1},{129,65},{193,129... | collective-permute-start | bytes 1572872 | tf_op jit(solution)/shard_map/ppermute | solution.py:309
  9.5 14.9 %collective-permute-start.7 = (f32[1,2,256,256]{3,2,1,0:T(8,128)S(1)}, f32[1,2,256,256]{3,2,1,0:T(8,128)S(1)}, u32[]{:S(2)}, u32[]{:S(2)}) collective-permute-start(f32[1,2,256,256]{3,2,1,0:T(8,128)S(1)} %get-tuple-element.38), channel_id=1, source_target_pairs={{0,64},{64,128},{128,192},{192,0},{1,65},{65,129},{129,193},{193,1... | collective-permute-start | bytes 1572872 | tf_op jit(solution)/shard_map/ppermute | solution.py:309
  10.1 23.6 %collective-permute-start.8 = (f32[1,2,256,256]{3,2,1,0:T(8,128)S(1)}, f32[1,2,256,256]{3,2,1,0:T(8,128)S(1)}, u32[]{:S(2)}, u32[]{:S(2)}) collective-permute-start(f32[1,2,256,256]{3,2,1,0:T(8,128)S(1)} %get-tuple-element.36), channel_id=1, source_target_pairs={{0,128},{64,192},{128,0},{192,64},{1,129},{65,193},{129,1},{193,65... | collective-permute-start | bytes 1572872 | tf_op jit(solution)/shard_map/ppermute | solution.py:309
  11.6 2.1 %collective-permute-start.4 = (f32[3,64,256]{2,1,0:T(8,128)S(1)}, f32[3,64,256]{2,1,0:T(8,128)S(1)}, u32[]{:S(2)}, u32[]{:S(2)}) collective-permute-start(f32[3,64,256]{2,1,0:T(8,128)S(1)} %constant_dynamic-update-slice_fusion.refs_5_), channel_id=1, source_target_pairs={{0,1},{1,0},{2,3},{3,2},{4,5},{5,4},{6,7},{7,6},{8,9},{9,8},{10,11... | collective-permute-start | bytes 589832 | tf_op jit(solution)/shard_map/ppermute | solution.py:334
  11.7 7.5 %collective-permute-start.5 = (f32[3,64,256]{2,1,0:T(8,128)S(1)}, f32[3,64,256]{2,1,0:T(8,128)S(1)}, u32[]{:S(2)}, u32[]{:S(2)}) collective-permute-start(f32[3,64,256]{2,1,0:T(8,128)S(1)} %constant_dynamic-update-slice_fusion.refs_5_), channel_id=1, source_target_pairs={{0,2},{1,3},{2,0},{3,1},{4,6},{5,7},{6,4},{7,5},{8,10},{9,11},{10,... | collective-permute-start | bytes 589832 | tf_op jit(solution)/shard_map/ppermute | solution.py:334
  13.7 6.9 %collective-permute-start.6 = (f32[3,64,256]{2,1,0:T(8,128)S(1)}, f32[3,64,256]{2,1,0:T(8,128)S(1)}, u32[]{:S(2)}, u32[]{:S(2)}) collective-permute-start(f32[3,64,256]{2,1,0:T(8,128)S(1)} %constant_dynamic-update-slice_fusion.refs_5_), channel_id=1, source_target_pairs={{0,17},{1,16},{2,19},{3,18},{4,21},{5,20},{6,23},{7,22},{8,25},{9,... | collective-permute-start | bytes 589832 | tf_op jit(solution)/shard_map/ppermute | solution.py:334
  14.2 1.6 %copy-start.1 = (f32[4,2,256,256]{3,2,1,0:T(8,128)S(1)}, f32[4,2,256,256]{3,2,1,0:T(8,128)}, u32[]{:S(2)}) copy-start(f32[4,2,256,256]{3,2,1,0:T(8,128)} %boundary_all.1) | copy-start | bytes 6291460
  15.8 7.3 %copy-start.2 = (f32[1,256,256]{2,1,0:T(8,128)S(1)}, f32[1,256,256]{2,1,0:T(8,128)}, u32[]{:S(2)}) copy-start(f32[1,256,256]{2,1,0:T(8,128)} %refs_3_.1) | copy-start | bytes 786436
  38.2 12.5 %collective-permute-start.9 = (f32[1,2,256,256]{3,2,1,0:T(8,128)S(1)}, f32[1,2,256,256]{3,2,1,0:T(8,128)S(1)}, u32[]{:S(2)}, u32[]{:S(2)}) collective-permute-start(f32[1,2,256,256]{3,2,1,0:T(8,128)S(1)} %get-tuple-element.27), channel_id=1, source_target_pairs={{0,64},{64,128},{128,192},{192,0},{1,65},{65,129},{129,193},{193,1... | collective-permute-start | bytes 1572872 | tf_op jit(solution)/shard_map/ppermute | solution.py:309
  39.3 12.2 %collective-permute-start.10 = (f32[1,2,256,256]{3,2,1,0:T(8,128)S(1)}, f32[1,2,256,256]{3,2,1,0:T(8,128)S(1)}, u32[]{:S(2)}, u32[]{:S(2)}) collective-permute-start(f32[1,2,256,256]{3,2,1,0:T(8,128)S(1)} %get-tuple-element.28), channel_id=1, source_target_pairs={{0,192},{64,0},{128,64},{192,128},{1,193},{65,1},{129,65},{193,129... | collective-permute-start | bytes 1572872 | tf_op jit(solution)/shard_map/ppermute | solution.py:309
  40.3 12.3 %collective-permute-start.11 = (f32[1,2,256,256]{3,2,1,0:T(8,128)S(1)}, f32[1,2,256,256]{3,2,1,0:T(8,128)S(1)}, u32[]{:S(2)}, u32[]{:S(2)}) collective-permute-start(f32[1,2,256,256]{3,2,1,0:T(8,128)S(1)} %get-tuple-element.26.refs_2_), channel_id=1, source_target_pairs={{1,0},{2,1},{3,2},{4,3},{5,4},{6,5},{7,6},{8,7},{9,8},{10,9},{11,1... | collective-permute-start | bytes 1572872 | tf_op jit(solution)/shard_map/ppermute | solution.py:318
  50.7 17.9 %copy-start.3 = (f32[1,6]{1,0:T(1,128)S(1)}, f32[1,6]{1,0:T(1,128)}, u32[]{:S(2)}) copy-start(f32[1,6]{1,0:T(1,128)} %param.9) | copy-start | bytes 76
  50.7 17.9 %copy-start.4 = (s32[6]{0:T(128)S(1)}, s32[6]{0:T(128)}, u32[]{:S(2)}) copy-start(s32[6]{0:T(128)} %param.8) | copy-start | bytes 76
  52.6 10.9 %collective-permute-start.14 = (f32[1,1,256,256]{3,2,1,0:T(8,128)S(1)}, f32[1,1,256,256]{3,2,1,0:T(8,128)S(1)}, u32[]{:S(2)}, u32[]{:S(2)}) collective-permute-start(f32[1,1,256,256]{3,2,1,0:T(8,128)S(1)} %get-tuple-element.31), channel_id=1, source_target_pairs={{0,128},{64,192},{128,0},{192,64},{1,129},{65,193},{129,1},{193,65... | collective-permute-start | bytes 786440 | tf_op jit(solution)/shard_map/ppermute | solution.py:309
  55.0 11.7 %collective-permute-start.15 = (f32[1,1,256,256]{3,2,1,0:T(8,128)S(1)}, f32[1,1,256,256]{3,2,1,0:T(8,128)S(1)}, u32[]{:S(2)}, u32[]{:S(2)}) collective-permute-start(f32[1,1,256,256]{3,2,1,0:T(8,128)S(1)} %get-tuple-element.32), channel_id=1, source_target_pairs={{0,128},{64,192},{128,0},{192,64},{1,129},{65,193},{129,1},{193,65... | collective-permute-start | bytes 786440 | tf_op jit(solution)/shard_map/ppermute | solution.py:309
  56.1 12.6 %collective-permute-start.12 = (f32[1,2,256,256]{3,2,1,0:T(8,128)S(1)}, f32[1,2,256,256]{3,2,1,0:T(8,128)S(1)}, u32[]{:S(2)}, u32[]{:S(2)}) collective-permute-start(f32[1,2,256,256]{3,2,1,0:T(8,128)S(1)} %admit.2.refs_3_), channel_id=1, source_target_pairs={{0,1},{1,2},{2,3},{3,4},{4,5},{5,6},{6,7},{7,8},{8,9},{9,10},{10,1... | collective-permute-start | bytes 1572872 | tf_op jit(solution)/shard_map/ppermute | solution.py:318
  61.5 12.6 %collective-permute-start.13 = (f32[1,2,256,256]{3,2,1,0:T(8,128)S(1)}, f32[1,2,256,256]{3,2,1,0:T(8,128)S(1)}, u32[]{:S(2)}, u32[]{:S(2)}) collective-permute-start(f32[1,2,256,256]{3,2,1,0:T(8,128)S(1)} %admit.3.refs_4_), channel_id=1, source_target_pairs={{1,0},{2,1},{3,2},{4,3},{5,4},{6,5},{7,6},{8,7},{9,8},{10,9},{11,1... | collective-permute-start | bytes 1572872 | tf_op jit(solution)/shard_map/ppermute | solution.py:318
  63.5 13.4 %collective-permute-start.16 = (f32[1,1,256,256]{3,2,1,0:T(8,128)S(1)}, f32[1,1,256,256]{3,2,1,0:T(8,128)S(1)}, u32[]{:S(2)}, u32[]{:S(2)}) collective-permute-start(f32[1,1,256,256]{3,2,1,0:T(8,128)S(1)} %collective-permute-done.14.refs_8_), channel_id=1, source_target_pairs={{0,1},{1,2},{2,3},{3,4},{4,5},{5,6},{6,7},{7,8},{8,9},{9,10},{10,1... | collective-permute-start | bytes 786440 | tf_op jit(solution)/shard_map/ppermute | solution.py:318
  66.7 13.0 %collective-permute-start.17 = (f32[1,1,256,256]{3,2,1,0:T(8,128)S(1)}, f32[1,1,256,256]{3,2,1,0:T(8,128)S(1)}, u32[]{:S(2)}, u32[]{:S(2)}) collective-permute-start(f32[1,1,256,256]{3,2,1,0:T(8,128)S(1)} %collective-permute-done.15.refs_9_), channel_id=1, source_target_pairs={{0,1},{1,2},{2,3},{3,4},{4,5},{5,6},{6,7},{7,8},{8,9},{9,10},{10,1... | collective-permute-start | bytes 786440 | tf_op jit(solution)/shard_map/ppermute | solution.py:318
